TPU v7x, 32 devices: a whole 2x2x4 slice. The times are simulated.
32 devices in a mesh: fsdp: 2 (over x), context: 8 (over z, core), tensor: 2 (over y).
Axes of the slice: x: 2, y: 2, z: 4, core: 2. Of those that a mesh axis runs over, the one named last changes fastest.
Arguments:
- layer_input: bfloat16 [4, 3072, 768], P('fsdp', 'context'), may hold values from -6 to 6
- attention_gain: bfloat16 [768], P('fsdp'), may hold values from 0.099609375 to 1.8984375
- attention_shift: bfloat16 [768], P('fsdp'), may hold values from -1.5 to 1.5
- query_key_value_weight: bfloat16 [768, 3, 768], P('fsdp', None, 'tensor'), may hold values from -0.21875 to 0.21875
- query_key_value_bias: bfloat16 [3, 12, 64], P(None, 'tensor', 'fsdp'), may hold values from -2.5 to 2.5
- attention_output_weight: bfloat16 [768, 768], P('tensor', 'fsdp'), may hold values from -1.25 to 1.25
- output_bias: bfloat16 [768], P('fsdp'), may hold values from -1.5 to 1.5
- feed_gain: bfloat16 [768], P('fsdp'), may hold values from 0.099609375 to 1.8984375
- feed_shift: bfloat16 [768], P('fsdp'), may hold values from -1.5 to 1.5
- up_projection_weight: bfloat16 [768, 3072], P('fsdp', 'tensor'), may hold values from -0.21875 to 0.21875
- up_projection_bias: bfloat16 [48, 64], P('tensor', 'fsdp'), may hold values from -2.5 to 2.5
- down_projection_weight: bfloat16 [3072, 768], P('tensor', 'fsdp'), may hold values from -0.109375 to 0.109375
- down_bias: bfloat16 [768], P('fsdp'), may hold values from -1.5 to 1.5
- cotangent: bfloat16 [4, 3072, 768], P('fsdp', 'context'), may hold values from -6 to 6
Outputs:
- layer_output: bfloat16 [4, 3072, 768], P('fsdp', 'context')
- input_grad: float32 [4, 3072, 768], P('fsdp', 'context')
- grad_attention_gain: float32 [768], P('fsdp')
- grad_attention_shift: float32 [768], P('fsdp')
- grad_heads_weight: float32 [768, 3, 768], P('fsdp', None, 'tensor')
- grad_heads_bias: float32 [3, 12, 64], P(None, 'tensor', 'fsdp')
- grad_output_weight: float32 [768, 768], P('tensor', 'fsdp')
- grad_output_bias: float32 [768], P('fsdp')
- grad_feed_gain: float32 [768], P('fsdp')
- grad_feed_shift: float32 [768], P('fsdp')
- grad_up_weight: float32 [768, 3072], P('fsdp', 'tensor')
- grad_up_bias: float32 [48, 64], P('tensor', 'fsdp')
- grad_down_weight: float32 [3072, 768], P('tensor', 'fsdp')
- grad_down_bias: float32 [768], P('fsdp')
All inputs are finite; a program needn't handle non-finite values.
Results may differ from a plain program's by a relative error of at most 0.025.
Values may be sent and summed in bfloat16 or wider, within the bound.
A program may use at most 384 MiB of HBM per device.

v0:
```python
import math

import jax
import jax.numpy as jnp
from jax import lax
from jax.sharding import PartitionSpec as P

HEAD_SIZE = 64
ROT = 16


norm_eps = 1e-05
rotary_base = 10000.0
masked_score = -1e30


def layer_norm(values, gain, shift):
    center = values - jnp.mean(values, axis=-1, keepdims=True)
    spread = jnp.mean(center * center, axis=-1, keepdims=True)
    return center * lax.rsqrt(spread + norm_eps) * gain + shift


def rotate(values, cosine, sine_table):
    half_dim = ROT // 2
    leading = values[..., :half_dim]
    trailing = values[..., half_dim:ROT]
    return jnp.concatenate(
        [
            leading * cosine - trailing * sine_table,
            trailing * cosine + leading * sine_table,
            values[..., ROT:],
        ],
        axis=-1,
    )


def arranged_position(member, within, block_rows, members):
    half_rows = block_rows // 2
    return jnp.where(
        within < half_rows,
        member * half_rows + within,
        (2 * members - 1 - member) * half_rows + within - half_rows,
    )


def per_device(
    layer_input,
    attention_gain,
    attention_shift,
    query_key_value_weight,
    query_key_value_bias,
    attention_output_weight,
    output_bias,
    feed_gain,
    feed_shift,
    up_projection_weight,
    up_projection_bias,
    down_projection_weight,
    down_bias,
    cotangent,
):
    gathered = (
        lax.all_gather(attention_gain, "fsdp", axis=0, tiled=True),
        lax.all_gather(attention_shift, "fsdp", axis=0, tiled=True),
        lax.all_gather(query_key_value_weight, "fsdp", axis=0, tiled=True),
        lax.all_gather(query_key_value_bias, "fsdp", axis=2, tiled=True),
        lax.all_gather(attention_output_weight, "fsdp", axis=1, tiled=True),
        lax.all_gather(output_bias, "fsdp", axis=0, tiled=True),
        lax.all_gather(feed_gain, "fsdp", axis=0, tiled=True),
        lax.all_gather(feed_shift, "fsdp", axis=0, tiled=True),
        lax.all_gather(up_projection_weight, "fsdp", axis=0, tiled=True),
        lax.all_gather(up_projection_bias, "fsdp", axis=1, tiled=True),
        lax.all_gather(down_projection_weight, "fsdp", axis=1, tiled=True),
        lax.all_gather(down_bias, "fsdp", axis=0, tiled=True),
    )
    (
        full_attention_gain,
        full_attention_shift,
        full_heads_weight,
        full_heads_bias,
        full_output_weight,
        full_output_bias,
        full_feed_gain,
        full_feed_shift,
        full_up_weight,
        full_up_bias,
        full_down_weight,
        full_down_bias,
    ) = gathered
    seq_count, row_count, model_width = layer_input.shape
    local_width = full_heads_weight.shape[2]
    local_heads = local_width // HEAD_SIZE
    members = lax.axis_size("context")
    member = lax.axis_index("context")
    inverse_root = 1.0 / math.sqrt(HEAD_SIZE)
    query_place = arranged_position(
        member, jnp.arange(row_count, dtype=jnp.int32), row_count, members
    )
    frequency = jnp.power(
        jnp.float32(rotary_base), -2.0 * jnp.arange(ROT // 2, dtype=jnp.float32) / ROT
    )
    phases = query_place.astype(jnp.float32)[:, None] * frequency[None, :]
    cosine = jnp.cos(phases)[:, None, :]
    sine_table = jnp.sin(phases)[:, None, :]
    inputs_float = layer_input.astype(jnp.float32)
    attention_gain_f = full_attention_gain.astype(jnp.float32)
    attention_shift_f = full_attention_shift.astype(jnp.float32)
    feed_gain_f = full_feed_gain.astype(jnp.float32)
    feed_shift_f = full_feed_shift.astype(jnp.float32)
    attention_normalized = layer_norm(inputs_float, attention_gain_f, attention_shift_f).astype(
        jnp.bfloat16
    )
    feed_normalized = layer_norm(inputs_float, feed_gain_f, feed_shift_f).astype(jnp.bfloat16)
    projected_heads = jnp.einsum(
        "std,dce->stce", attention_normalized, full_heads_weight, preferred_element_type=jnp.float32
    ) + full_heads_bias.astype(jnp.float32).reshape(3, local_width)
    head_shape = (seq_count, row_count, local_heads, HEAD_SIZE)
    query_bf = rotate(projected_heads[:, :, 0].reshape(head_shape), cosine, sine_table).astype(
        jnp.bfloat16
    )
    keys_bf = (
        rotate(projected_heads[:, :, 1].reshape(head_shape), cosine, sine_table)
        .astype(jnp.bfloat16)
        .reshape(seq_count, row_count, local_width)
    )
    values_bf = projected_heads[:, :, 2].astype(jnp.bfloat16)

    def scores_for(key_piece):
        piece_rows = key_piece.shape[1]
        key_heads = key_piece.reshape(seq_count, piece_rows, local_heads, HEAD_SIZE)
        scores = (
            jnp.einsum("sqhd,skhd->shqk", query_bf, key_heads, preferred_element_type=jnp.float32)
            * inverse_root
        )
        row_numbers = jnp.arange(piece_rows, dtype=jnp.int32)
        key_place = arranged_position(
            row_numbers // row_count, row_numbers % row_count, row_count, members
        )
        allowed = key_place[None, :] <= query_place[:, None]
        return (scores, allowed, key_heads)

    old_max = jnp.full((seq_count, local_heads, row_count), masked_score, jnp.float32)
    key_piece = lax.all_gather(keys_bf, "context", axis=1, tiled=True)
    value_piece = lax.all_gather(values_bf, "context", axis=1, tiled=True)
    piece_rows = key_piece.shape[1]
    scores, allowed, key_heads = scores_for(key_piece)
    new_max = jnp.maximum(old_max, jnp.max(jnp.where(allowed, scores, masked_score), axis=-1))
    weights = jnp.where(allowed, jnp.exp(scores - new_max[..., None]), 0.0)
    value_heads = value_piece.reshape(seq_count, piece_rows, local_heads, HEAD_SIZE)
    weighted = jnp.einsum(
        "shqk,skhd->shqd",
        weights.astype(jnp.bfloat16),
        value_heads,
        preferred_element_type=jnp.float32,
    )
    statistics = (new_max, jnp.sum(weights, axis=-1), weighted)
    row_max, row_total, weighted = statistics
    attention_mixed = weighted / row_total[..., None]
    log_total = row_max + jnp.log(row_total)
    attended_bf = (
        jnp.transpose(attention_mixed, (0, 2, 1, 3))
        .reshape(seq_count, row_count, local_width)
        .astype(jnp.bfloat16)
    )
    hidden_units = jnp.einsum(
        "std,df->stf", feed_normalized, full_up_weight, preferred_element_type=jnp.float32
    ) + full_up_bias.astype(jnp.float32).reshape(-1)
    gelu_output, gelu_back = jax.vjp(
        lambda argument: jax.nn.gelu(argument, approximate=False), hidden_units
    )
    activated_bf = gelu_output.astype(jnp.bfloat16)
    partial_terms = jnp.einsum(
        "ste,ed->std", attended_bf, full_output_weight, preferred_element_type=jnp.float32
    ) + jnp.einsum(
        "stf,fd->std", activated_bf, full_down_weight, preferred_element_type=jnp.float32
    )
    branches = lax.psum(partial_terms.astype(jnp.bfloat16), "tensor").astype(jnp.float32)
    layer_output = (
        inputs_float
        + branches
        + full_output_bias.astype(jnp.float32)
        + full_down_bias.astype(jnp.float32)
    ).astype(jnp.bfloat16)
    attended_grad = jnp.einsum(
        "std,ed->ste", cotangent, full_output_weight, preferred_element_type=jnp.float32
    ).astype(jnp.bfloat16)
    grad_heads4 = attended_grad.reshape(head_shape)
    row_dot = jnp.sum(
        jnp.transpose(grad_heads4.astype(jnp.float32), (0, 2, 1, 3)) * attention_mixed, axis=-1
    )
    activated_grad = jnp.einsum(
        "std,fd->stf", cotangent, full_down_weight, preferred_element_type=jnp.float32
    )
    hidden_grad = gelu_back(activated_grad)[0].astype(jnp.bfloat16)
    output_weight_grad = jnp.einsum(
        "ste,std->ed", attended_bf, cotangent, preferred_element_type=jnp.float32
    )
    down_weight_grad = jnp.einsum(
        "stf,std->fd", activated_bf, cotangent, preferred_element_type=jnp.float32
    )
    bias_total = jnp.sum(cotangent.astype(jnp.float32), axis=(0, 1))
    up_weight_grad = jnp.einsum(
        "std,stf->df", feed_normalized, hidden_grad, preferred_element_type=jnp.float32
    )
    up_bias_grad = jnp.sum(hidden_grad.astype(jnp.float32), axis=(0, 1)).reshape(full_up_bias.shape)
    feed_part = jnp.einsum(
        "stf,df->std", hidden_grad, full_up_weight, preferred_element_type=jnp.float32
    )
    key_piece = lax.all_gather(keys_bf, "context", axis=1, tiled=True)
    value_piece = lax.all_gather(values_bf, "context", axis=1, tiled=True)
    piece_rows = key_piece.shape[1]
    scores, allowed, key_heads = scores_for(key_piece)
    probabilities = jnp.where(allowed, jnp.exp(scores - log_total[..., None]), 0.0)
    value_heads = value_piece.reshape(seq_count, piece_rows, local_heads, HEAD_SIZE)
    prob_grad = jnp.einsum(
        "sqhd,skhd->shqk", grad_heads4, value_heads, preferred_element_type=jnp.float32
    )
    score_grad = (probabilities * (prob_grad - row_dot[..., None])).astype(jnp.bfloat16)
    query_grad = (
        jnp.einsum("shqk,skhd->shqd", score_grad, key_heads, preferred_element_type=jnp.float32)
        * inverse_root
    )
    key_part = (
        jnp.einsum("shqk,sqhd->skhd", score_grad, query_bf, preferred_element_type=jnp.float32)
        * inverse_root
    )
    value_part = jnp.einsum(
        "shqk,sqhd->skhd",
        probabilities.astype(jnp.bfloat16),
        grad_heads4,
        preferred_element_type=jnp.float32,
    )
    key_grads = key_part.reshape(seq_count, piece_rows, local_width)
    value_grads = value_part.reshape(seq_count, piece_rows, local_width)
    attention_grads = (query_grad, key_grads, value_grads)
    query_grad, key_grads, value_grads = attention_grads
    own_keys, own_values = (
        lax.psum_scatter(
            key_grads.astype(jnp.bfloat16), "context", scatter_dimension=1, tiled=True
        ).astype(jnp.float32),
        lax.psum_scatter(
            value_grads.astype(jnp.bfloat16), "context", scatter_dimension=1, tiled=True
        ).astype(jnp.float32),
    )
    query_back = rotate(jnp.transpose(query_grad, (0, 2, 1, 3)), cosine, -sine_table).reshape(
        seq_count, row_count, local_width
    )
    key_back = rotate(own_keys.reshape(head_shape), cosine, -sine_table).reshape(
        seq_count, row_count, local_width
    )
    projected_grad = jnp.stack([query_back, key_back, own_values], axis=2).astype(jnp.bfloat16)
    heads_weight_grad = jnp.einsum(
        "std,stce->dce", attention_normalized, projected_grad, preferred_element_type=jnp.float32
    )
    heads_bias_grad = jnp.sum(projected_grad.astype(jnp.float32), axis=(0, 1)).reshape(
        3, local_heads, HEAD_SIZE
    )
    heads_part = jnp.einsum(
        "stce,dce->std", projected_grad, full_heads_weight, preferred_element_type=jnp.float32
    )
    attention_normed_grad, feed_normed_grad = (
        lax.psum(heads_part.astype(jnp.bfloat16), "tensor").astype(jnp.float32),
        lax.psum(feed_part.astype(jnp.bfloat16), "tensor").astype(jnp.float32),
    )
    unused_first, attention_back = jax.vjp(
        layer_norm, inputs_float, attention_gain_f, attention_shift_f
    )
    input_part_a, first_gain_grad, first_shift_grad = attention_back(attention_normed_grad)
    unused_second, feed_back = jax.vjp(layer_norm, inputs_float, feed_gain_f, feed_shift_f)
    input_part_f, second_gain_grad, second_shift_grad = feed_back(feed_normed_grad)
    input_grad = cotangent.astype(jnp.float32) + input_part_a + input_part_f
    summed = (
        lax.psum(first_gain_grad.astype(jnp.bfloat16), "context").astype(jnp.float32),
        lax.psum(first_shift_grad.astype(jnp.bfloat16), "context").astype(jnp.float32),
        lax.psum(heads_weight_grad.astype(jnp.bfloat16), "context").astype(jnp.float32),
        lax.psum(heads_bias_grad.astype(jnp.bfloat16), "context").astype(jnp.float32),
        lax.psum(output_weight_grad.astype(jnp.bfloat16), "context").astype(jnp.float32),
        lax.psum(bias_total.astype(jnp.bfloat16), "context").astype(jnp.float32),
        lax.psum(second_gain_grad.astype(jnp.bfloat16), "context").astype(jnp.float32),
        lax.psum(second_shift_grad.astype(jnp.bfloat16), "context").astype(jnp.float32),
        lax.psum(up_weight_grad.astype(jnp.bfloat16), "context").astype(jnp.float32),
        lax.psum(up_bias_grad.astype(jnp.bfloat16), "context").astype(jnp.float32),
        lax.psum(down_weight_grad.astype(jnp.bfloat16), "context").astype(jnp.float32),
        lax.psum(bias_total.astype(jnp.bfloat16), "context").astype(jnp.float32),
    )
    results = (
        lax.psum_scatter(
            summed[0].astype(jnp.bfloat16), "fsdp", scatter_dimension=0, tiled=True
        ).astype(jnp.float32),
        lax.psum_scatter(
            summed[1].astype(jnp.bfloat16), "fsdp", scatter_dimension=0, tiled=True
        ).astype(jnp.float32),
        lax.psum_scatter(
            summed[2].astype(jnp.bfloat16), "fsdp", scatter_dimension=0, tiled=True
        ).astype(jnp.float32),
        lax.psum_scatter(
            summed[3].astype(jnp.bfloat16), "fsdp", scatter_dimension=2, tiled=True
        ).astype(jnp.float32),
        lax.psum_scatter(
            summed[4].astype(jnp.bfloat16), "fsdp", scatter_dimension=1, tiled=True
        ).astype(jnp.float32),
        lax.psum_scatter(
            summed[5].astype(jnp.bfloat16), "fsdp", scatter_dimension=0, tiled=True
        ).astype(jnp.float32),
        lax.psum_scatter(
            summed[6].astype(jnp.bfloat16), "fsdp", scatter_dimension=0, tiled=True
        ).astype(jnp.float32),
        lax.psum_scatter(
            summed[7].astype(jnp.bfloat16), "fsdp", scatter_dimension=0, tiled=True
        ).astype(jnp.float32),
        lax.psum_scatter(
            summed[8].astype(jnp.bfloat16), "fsdp", scatter_dimension=0, tiled=True
        ).astype(jnp.float32),
        lax.psum_scatter(
            summed[9].astype(jnp.bfloat16), "fsdp", scatter_dimension=1, tiled=True
        ).astype(jnp.float32),
        lax.psum_scatter(
            summed[10].astype(jnp.bfloat16), "fsdp", scatter_dimension=1, tiled=True
        ).astype(jnp.float32),
        lax.psum_scatter(
            summed[11].astype(jnp.bfloat16), "fsdp", scatter_dimension=0, tiled=True
        ).astype(jnp.float32),
    )
    return (
        layer_output,
        input_grad,
        results[0],
        results[1],
        results[2],
        results[3],
        results[4],
        results[5],
        results[6],
        results[7],
        results[8],
        results[9],
        results[10],
        results[11],
    )


def solution(mesh):
    in_specs = (
        P("fsdp", "context", None),
        P("fsdp"),
        P("fsdp"),
        P("fsdp", None, "tensor"),
        P(None, "tensor", "fsdp"),
        P("tensor", "fsdp"),
        P("fsdp"),
        P("fsdp"),
        P("fsdp"),
        P("fsdp", "tensor"),
        P("tensor", "fsdp"),
        P("tensor", "fsdp"),
        P("fsdp"),
        P("fsdp", "context", None),
    )
    out_specs = (
        P("fsdp", "context", None),
        P("fsdp", "context", None),
        P("fsdp"),
        P("fsdp"),
        P("fsdp", None, "tensor"),
        P(None, "tensor", "fsdp"),
        P("tensor", "fsdp"),
        P("fsdp"),
        P("fsdp"),
        P("fsdp"),
        P("fsdp", "tensor"),
        P("tensor", "fsdp"),
        P("tensor", "fsdp"),
        P("fsdp"),
    )
    return jax.shard_map(
        per_device, mesh=mesh, in_specs=in_specs, out_specs=out_specs, check_vma=False
    )
```

profile of v0, /device:TPU:0, one launch (start us, length us, event | category | flops | bytes accessed | tf_op | source)
XLA Modules:
  0.0 706.2 jit_solution(7148360093825466325)
XLA Ops:
  7.3 2.4 copy.74
  9.7 5.2 all-gather.1
  15.0 4.3 all-gather.2
  19.5 4.9 all_gather.47
  26.1 16.6 %all-gather.14.cloned.1.call-done = bf16[768,3,384]{0,2,1:T(8,128)(2,1)} async-done(((bf16[384,3,384]{0,2,1:T(8,128)(2,1)}), bf16[768,3,384]{0,2,1:T(8,128)(2,1)}) %all-gather.14.cloned.1.call-update) | async-done | bytes 1769488 | tf_op jit(solution)/shard_map/all_gather | solution.py:65
  42.7 3.2 convolution_add_fusion
  46.1 1.6 copy-done.8
  49.8 2.2 slice.100
  53.3 9.4 %all_gather.50 = bf16[384,768]{1,0:T(8,128)(2,1)S(1)} all-gather(bf16[384,384]{1,0:T(8,128)(2,1)S(1)} %copy-done.18), channel_id=1, replica_groups=mesh['fsdp'=2,'context'=8,'tensor'=2] {'fsdp'}, dimensions={1}, use_global_device_ids=true | all-gather | bytes 884736 | tf_op jit(solution)/shard_map/all_gather | solution.py:67
  63.6 1.5 convolution_convert_fusion
  65.0 2.0 slice.103
  67.0 34.4 %all-gather.16.cloned.1.call-done = bf16[2,3072,384]{1,2,0:T(8,128)(2,1)} async-done(((bf16[2,384,384]{1,2,0:T(8,128)(2,1)}), bf16[2,3072,384]{1,2,0:T(8,128)(2,1)}) %all-gather.16.cloned.1.call-update) | async-done | bytes 4718608 | tf_op jit(solution)/shard_map/all_gather | solution.py:143
  101.4 24.4 %select_reduce_fusion = (f32[2,6,384]{2,1,0:T(8,128)S(1)}, f32[2,6,384,3072]{3,2,1,0:T(8,128)}) fusion(pred[384,3072]{1,0:T(8,128)(4,1)S(1)} %broadcast_compare_fusion, bf16[2,3072,6,64]{1,3,2,0:T(8,128)(2,1)} %bitcast.120, bf16[2,384,6,48]{1,3,2,0:T(8,128)(2,1)} %slice.103, bf16[2,384,6,8]{1,3,2,0:T(8,128)(2,1)} %get-tuple-element.54, ...), kind=kOutput, calls=%fused_computation.3 | convolution fusion | flops 1856171520 | bytes 63129600 | tf_op jit(solution)/shard_map/sqhd,skhd->shqk/dot_general | solution.py:132
  127.0 21.5 %fusion = f32[2,6,384]{2,1,0:T(8,128)} fusion(f32[2,6,384,3072]{3,2,1,0:T(8,128)} %get-tuple-element.68, f32[2,6,384]{2,1,0:T(8,128)} %broadcast_maximum_fusion, pred[384,3072]{1,0:T(8,128)(4,1)S(1)} %broadcast_compare_fusion), kind=kLoop, calls=%fused_computation.4 | loop fusion | flops 56618496 | bytes 57839616 | tf_op jit(solution)/shard_map/reduce_sum | solution.py:156
  148.6 1.4 log_add_fusion
  149.9 3.9 all-gather.22.cloned.1.call-done
  153.9 26.3 %fusion.63 = (bf16[2,384,6,64]{1,3,2,0:T(8,128)(2,1)}, f32[2,6,384,64]{2,3,1,0:T(8,128)S(1)}) fusion(f32[2,384,6]{1,2,0:T(8,128)} %bitcast.149, bf16[2,3072,6,64]{1,3,2,0:T(8,128)(2,1)} %bitcast.155, f32[2,6,384,3072]{3,2,1,0:T(8,128)} %get-tuple-element.68, f32[2,6,384]{2,1,0:T(8,128)} %broadcast_maximum_fusion, ...), kind=kOutput, calls=%fused_computation.97 | convolution fusion | flops 1869152256 | bytes 64327680 | tf_op jit(solution)/shard_map/shqk,skhd->shqd/dot_general | solution.py:150
  181.6 34.7 %multiply_convert_fusion = bf16[2,6,384,3072]{3,2,1,0:T(8,128)(2,1)} fusion(f32[2,6,384,3072]{3,2,1,0:T(8,128)} %get-tuple-element.68, f32[2,6,384]{2,1,0:T(8,128)S(1)} %fusion.62, f32[2,6,384]{2,1,0:T(8,128)S(1)} %copy-done.36, pred[384,3072]{1,0:T(8,128)(4,1)S(1)} %broadcast_compare_fusion, bf16[2,384,6,64]{1,3,2,0:T(8,128)(2,1)} %bitcast.142, ...), kind=kOutput, calls=%fused_computation | convolution fusion | flops 1896873984 | bytes 91459584 | tf_op jit(solution)/shard_map/sqhd,skhd->shqk/dot_general | solution.py:215
  216.2 14.6 %multiply_convert_fusion.1 = bf16[2,6,64,3072]{3,2,1,0:T(8,128)(2,1)} fusion(bf16[2,6,384,3072]{3,2,1,0:T(8,128)(2,1)} %multiply_convert_fusion, bf16[2,384,6,48]{1,3,2,0:T(8,128)(2,1)S(1)} %copy-done.5, bf16[2,384,6,8]{1,3,2,0:T(8,128)(2,1)S(1)} %copy-done.16, bf16[2,384,6,8]{1,3,2,0:T(8,128)(2,1)S(1)} %copy-done.15), kind=kOutput, calls=%fused_computation.11 | convolution fusion | flops 1818427392 | bytes 33619968 | tf_op jit(solution)/shard_map/shqk,sqhd->skhd/dot_general | solution.py:224
  230.8 12.6 %copy.97 = bf16[2,3072,384]{2,0,1:T(2,128)(2,1)} copy(bf16[2,3072,384]{1,2,0:T(8,128)(2,1)} %bitcast.124) | data formatting | bytes 9437184
  243.4 5.3 copy.107
  248.8 24.6 %fusion.9 = bf16[2,6,64,3072]{3,2,1,0:T(8,128)(2,1)} fusion(bf16[2,384,6,64]{1,3,2,0:T(8,128)(2,1)} %bitcast.143, f32[2,6,384,3072]{3,2,1,0:T(8,128)} %get-tuple-element.68, f32[2,6,384]{2,1,0:T(8,128)} %log_add_fusion, pred[384,3072]{1,0:T(8,128)(4,1)S(1)} %broadcast_compare_fusion), kind=kOutput, calls=%fused_computation.13 | convolution fusion | flops 1870921728 | bytes 63129600 | tf_op jit(solution)/shard_map/shqk,sqhd->skhd/dot_general | solution.py:227
  273.4 6.7 copy.79
  280.7 4.3 all-gather.3
  285.1 4.4 all-gather.5
  289.7 4.3 all-gather.4
  294.1 5.1 fusion.65
  299.2 2.2 copy-done.4
  301.4 12.2 %multiply_convert_fusion.2 = (bf16[2,384,1536]{2,1,0:T(8,128)(2,1)}, f32[2,384,1536]{2,1,0:T(8,128)}) fusion(f32[2,384,1536]{2,1,0:T(8,128)S(1)} %get-tuple-element.66, f32[1536]{0:T(1024)S(1)} %reshape.254, u8[384,1536]{1,0:T(8,128)(4,1)S(1)} %get-tuple-element.15, u8[384,1536]{1,0:T(8,128)(4,1)S(1)} %get-tuple-element.14), kind=kLoop, calls=%fused_computation.23 | loop fusion | flops 83755008 | bytes 12982272 | tf_op jit(solution)/shard_map/convert_element_type | solution.py:171
  313.6 7.6 %fusion.97 = (bf16[1536]{0:T(1024)(128)(2,1)S(1)}, bf16[2,384,1536]{2,1,0:T(8,128)(2,1)}) fusion(f32[2,384,1536]{2,1,0:T(8,128)} %get-tuple-element.46, bf16[2,384,768]{2,1,0:T(8,128)(2,1)S(1)} %copy-done.3, bf16[1536,768]{1,0:T(8,128)(2,1)} %all-gather.20.cloned.1.call-done, f32[2,384,1536]{2,1,0:T(8,128)} %copy-done.4, f32[1536]{0:T(1024)S(1)} %reshape.254), kind=kOutput, calls=%fused_computation.165 | convolution fusion | flops 1830812160 | bytes 15344640 | tf_op jit(solution)/shard_map/std,fd->stf/dot_general | solution.py:191
  322.1 5.2 bitcast_convert_fusion
  327.2 4.3 copy.105
  331.7 6.0 fusion.43
  337.6 3.1 fusion.54
  342.5 16.1 %fusion.59 = f32[2,384,6,64]{1,3,2,0:T(8,128)S(1)} fusion(bf16[2,6,384,3072]{3,2,1,0:T(8,128)(2,1)} %multiply_convert_fusion, bf16[2,3072,6,64]{1,3,2,0:T(8,128)(2,1)} %bitcast.121), kind=kOutput, calls=%fused_computation.89 | convolution fusion | flops 1812234240 | bytes 34209792 | tf_op jit(solution)/shard_map/shqk,skhd->shqd/dot_general | solution.py:220
  360.4 1.8 add_convert_fusion.1
  362.3 1.8 reshape.291
  368.2 1.4 copy.81
  369.6 1.5 fusion.94
  372.0 1.5 reshape.292
  373.6 4.4 bitcast_convert_fusion.3
  378.7 5.4 bitcast_convert_fusion.1
  384.7 4.2 bitcast_convert_fusion.2
  389.9 4.3 all-gather.6
  394.8 4.3 all-gather.7
  401.1 1.4 copy.104
  402.4 4.1 reduce-scatter.33.cloned.1.call-done
  406.6 2.6 copy.106
  409.2 14.9 %reduce-scatter.29.cloned.1.call-done = bf16[384,384]{1,0:T(8,128)(2,1)} async-done(((bf16[768,384]{1,0:T(8,128)(2,1)}), bf16[384,384]{1,0:T(8,128)(2,1)}) %reduce-scatter.29.cloned.1.call-update) | async-done | bytes 294928
  424.1 1.8 copy.102
  425.9 10.2 %reduce-scatter.27.cloned.1.call-done = bf16[32,18]{1,0:T(8,128)(2,1)} async-done(((bf16[64,18]{1,0:T(8,128)(2,1)}), bf16[32,18]{1,0:T(8,128)(2,1)}) %reduce-scatter.27.cloned.1.call-update) | async-done | bytes 1168
  437.6 96.7 %all-reduce.14.cloned.1.call-done = (bf16[2,384,768]{2,1,0:T(8,128)(2,1)}, bf16[2,384,768]{2,1,0:T(8,128)(2,1)}, bf16[2,384,768]{2,1,0:T(8,128)(2,1)}) async-done(((bf16[2,384,768]{2,1,0:T(8,128)(2,1)}, bf16[2,384,768]{2,1,0:T(8,128)(2,1)}, bf16[2,384,768]{2,1,0:T(8,128)(2,1)}), (bf16[2,384,768]{2,1,0:T(8,128)(2,1)}, bf16[2,384,768]{2,1,0:T(8,128)(2,1)}, ...) | async-done | bytes 3538960 | tf_op jit(solution)/shard_map/psum | solution.py:177
  534.3 2.2 reduce_sum.174
  536.5 2.1 reduce_sum.181
  538.6 1.6 fusion.37
  540.8 31.1 %reduce-scatter.23.cloned.1.call-done = bf16[384,1536]{1,0:T(8,128)(2,1)} async-done(((bf16[768,1536]{1,0:T(8,128)(2,1)}), bf16[384,1536]{1,0:T(8,128)(2,1)}) %reduce-scatter.23.cloned.1.call-update) | async-done | bytes 1179664 | tf_op jit(solution)/shard_map/reduce_scatter | solution.py:311
  571.9 31.0 %reduce-scatter.21.cloned.1.call-done = bf16[384,3,384]{2,0,1:T(8,128)(2,1)} async-done(((bf16[768,3,384]{2,0,1:T(8,128)(2,1)}), bf16[384,3,384]{2,0,1:T(8,128)(2,1)}) %reduce-scatter.21.cloned.1.call-update) | async-done | bytes 884752 | tf_op jit(solution)/shard_map/reduce_scatter | solution.py:293
  604.2 3.8 fusion.35
  608.0 8.2 %all-reduce.8 = (bf16[768]{0:T(1024)(128)(2,1)}, bf16[768]{0:T(1024)(128)(2,1)}, bf16[768]{0:T(1024)(128)(2,1)}, bf16[768]{0:T(1024)(128)(2,1)}, bf16[768]{0:T(1024)(128)(2,1)}) all-reduce(bf16[768]{0:T(1024)(128)(2,1)} %get-tuple-element.21, ...), channel_id=5, replica_groups=mesh['fsdp'=2,'context'=8,'tensor'=2] {'fsdp'}, use_global_device_ids=true, to_apply=%region_16.17.clone | all-reduce | flops 3840 | bytes 15360
  622.8 30.0 %all-reduce.5 = (bf16[384]{0:T(512)(128)(2,1)}, bf16[384]{0:T(512)(128)(2,1)}, bf16[3,6,32]{2,1,0:T(8,128)(2,1)}, bf16[384]{0:T(512)(128)(2,1)}, bf16[384]{0:T(5...) all-reduce(bf16[384]{0:T(512)(128)(2,1)} %dynamic-slice.1, ...), channel_id=1, replica_groups=mesh['fsdp'=2,'context'=8,'tensor'=2] {'context'}, use_global_device_ids=true, to_apply=%region_15.16 | all-reduce | flops 3264 | bytes 13056 | tf_op jit(solution)/shard_map/psum | solution.py:273
  663.0 4.5 add_add_fusion.2
  667.5 24.5 %all-reduce.12.cloned.1.call-done = (bf16[384,3,384]{2,0,1:T(8,128)(2,1)}, bf16[384,384]{1,0:T(8,128)(2,1)}, bf16[384,1536]{1,0:T(8,128)(2,1)}, bf16[1536,384]{1,0:T(8,128)(2,1)}) async-done(((bf16[384,3,384]{2,0,1:T(8,128)(2,1)}, bf16[384,384]{1,0:T(8,128)(2,1)}, bf16[384,1536]{1,0:T(8,128)(2,1)}, bf16[1536,384]{1,0:T(8,128)(2,1)}), (bf16[384,3,384]{2,0,1:T(8,128)(2,1)}, bf16[384,384]{1,0:T(8,128)(2,1)}, ...) | async-done | bytes 3538960 | tf_op jit(solution)/shard_map/psum | solution.py:275
  692.0 3.1 convert_element_type.255
  695.1 1.6 convert_element_type.259
  (213 shorter events, 46.4 us)
Async XLA Ops:
  7.2 2.5 copy-start.43
  7.2 7.8 %copy-start.44 = (bf16[384]{0:T(512)(128)(2,1)S(1)}, bf16[384]{0:T(512)(128)(2,1)}, u32[]{:S(2)}) copy-start(bf16[384]{0:T(512)(128)(2,1)} %param.16) | copy-start | bytes 2308
  7.2 12.2 %copy-start.38 = (bf16[3,6,32]{2,1,0:T(8,128)(2,1)S(1)}, bf16[3,6,32]{2,1,0:T(8,128)(2,1)}, u32[]{:S(2)}) copy-start(bf16[3,6,32]{2,1,0:T(8,128)(2,1)} %param.18) | copy-start | bytes 3460
  7.2 17.4 %copy-start = (bf16[2,384,768]{2,1,0:T(8,128)(2,1)S(1)}, bf16[2,384,768]{2,1,0:T(8,128)(2,1)}, u32[]{:S(2)}) copy-start(bf16[2,384,768]{2,1,0:T(8,128)(2,1)} %param.14) | copy-start | bytes 3538948
  7.2 35.5 %all-gather.14.cloned.1.call-start = ((), (), s32[]{:S(2)}) async-start(), calls=%async_computation.8 | async-start | bytes 2654208 | tf_op jit(solution)/shard_map/all_gather | solution.py:65
  9.7 91.8 %all-gather.16.cloned.1.call-start = ((), (), s32[]{:S(2)}) async-start(), calls=%async_computation.9 | async-start | bytes 5308416 | tf_op jit(solution)/shard_map/all_gather | solution.py:143
  15.0 30.9 %copy-start.24 = (f32[768]{0:T(1024)}, f32[768]{0:T(1024)S(1)}, u32[]{:S(2)}) copy-start(f32[768]{0:T(1024)S(1)} %reshape.271) | copy-start | bytes 9220
  19.4 26.5 %copy-start.40 = (f32[768]{0:T(1024)}, f32[768]{0:T(1024)S(1)}, u32[]{:S(2)}) copy-start(f32[768]{0:T(1024)S(1)} %reshape.272) | copy-start | bytes 9220
  25.4 20.5 %copy-start.29 = (f32[2,384]{1,0:T(2,128)}, f32[2,384]{1,0:T(2,128)S(1)}, u32[]{:S(2)}) copy-start(f32[2,384]{1,0:T(2,128)S(1)} %fusion.36) | copy-start | bytes 9220
  25.4 20.5 %copy-start.31 = (f32[2,384]{1,0:T(2,128)}, f32[2,384]{1,0:T(2,128)S(1)}, u32[]{:S(2)}) copy-start(f32[2,384]{1,0:T(2,128)S(1)} %fusion.86) | copy-start | bytes 9220
  26.1 21.6 %copy-start.22 = (f32[384,8]{0,1:T(8,128)}, f32[384,8]{0,1:T(8,128)S(1)}, u32[]{:S(2)}) copy-start(f32[384,8]{0,1:T(8,128)S(1)} %get-tuple-element.65) | copy-start | bytes 36868
  45.9 1.7 copy-start.8
  46.1 2.0 copy-start.7
  49.7 3.6 copy-start.18
  49.8 104.1 %all-gather.22.cloned.1.call-start = ((), (), s32[]{:S(2)}) async-start(), calls=%async_computation.13 | async-start | bytes 5308416 | tf_op jit(solution)/shard_map/all_gather | solution.py:144
  52.0 11.5 %copy-start.3 = (bf16[2,384,768]{2,1,0:T(8,128)(2,1)S(1)}, bf16[2,384,768]{2,1,0:T(8,128)(2,1)}, u32[]{:S(2)}) copy-start(bf16[2,384,768]{2,1,0:T(8,128)(2,1)} %param.27) | copy-start | bytes 3538948
  52.0 242.0 %all-gather.18.cloned.1.call-start = ((), (), s32[]{:S(2)}) async-start(), calls=%async_computation.10 | async-start | bytes 3538944 | tf_op jit(solution)/shard_map/all_gather | solution.py:71
  52.6 261.0 %all-gather.20.cloned.1.call-start = ((), (), s32[]{:S(2)}) async-start(), calls=%async_computation.11 | async-start | bytes 3538944 | tf_op jit(solution)/shard_map/all_gather | solution.py:73
  53.2 309.1 %reduce-scatter.25.cloned.1.call-start = ((), (), s32[]{:S(2)}) async-start(), calls=%async_computation.16 | async-start | bytes 5308416
  62.7 0.8 copy-start.9
  153.9 26.4 %copy-start.20 = (f32[2,6,384]{2,1,0:T(8,128)S(1)}, f32[2,6,384]{2,1,0:T(8,128)}, u32[]{:S(2)}) copy-start(f32[2,6,384]{2,1,0:T(8,128)} %fusion) | copy-start | bytes 55300
  153.9 27.7 %copy-start.36 = (f32[2,6,384]{2,1,0:T(8,128)S(1)}, f32[2,6,384]{2,1,0:T(8,128)}, u32[]{:S(2)}) copy-start(f32[2,6,384]{2,1,0:T(8,128)} %log_add_fusion) | copy-start | bytes 55300
  181.5 34.7 %copy-start.5 = (bf16[2,384,6,48]{1,3,2,0:T(8,128)(2,1)S(1)}, bf16[2,384,6,48]{1,3,2,0:T(8,128)(2,1)}, u32[]{:S(2)}) copy-start(bf16[2,384,6,48]{1,3,2,0:T(8,128)(2,1)} %slice.103) | copy-start | bytes 1327108
  181.5 34.7 %copy-start.15 = (bf16[2,384,6,8]{1,3,2,0:T(8,128)(2,1)S(1)}, bf16[2,384,6,8]{1,3,2,0:T(8,128)(2,1)}, u32[]{:S(2)}) copy-start(bf16[2,384,6,8]{1,3,2,0:T(8,128)(2,1)} %get-tuple-element.53) | copy-start | bytes 221188
  181.6 34.7 %copy-start.16 = (bf16[2,384,6,8]{1,3,2,0:T(8,128)(2,1)S(1)}, bf16[2,384,6,8]{1,3,2,0:T(8,128)(2,1)}, u32[]{:S(2)}) copy-start(bf16[2,384,6,8]{1,3,2,0:T(8,128)(2,1)} %get-tuple-element.54) | copy-start | bytes 221188
  248.7 120.9 %reduce-scatter.19.cloned.1.call-start = ((), (), s32[]{:S(2)}) async-start(), calls=%async_computation.12 | async-start | bytes 5308416 | tf_op jit(solution)/shard_map/reduce_scatter | solution.py:241
  280.1 0.7 copy-start.45
  280.1 5.0 copy-start.39
  280.1 9.6 %copy-start.46 = (bf16[384]{0:T(512)(128)(2,1)S(1)}, bf16[384]{0:T(512)(128)(2,1)}, u32[]{:S(2)}) copy-start(bf16[384]{0:T(512)(128)(2,1)} %param.22) | copy-start | bytes 2308
  280.1 14.0 %copy-start.32 = (f32[2,384]{1,0:T(2,128)S(1)}, f32[2,384]{1,0:T(2,128)}, u32[]{:S(2)}) copy-start(f32[2,384]{1,0:T(2,128)} %copy-done.31) | copy-start | bytes 9220
  280.1 121.0 %reduce-scatter.31.cloned.1.call-start = ((), (), s32[]{:S(2)}) async-start(), calls=%async_computation.19 | async-start | bytes 24576
  285.1 14.0 %copy-start.26 = (f32[768]{0:T(1024)}, f32[768]{0:T(1024)S(1)}, u32[]{:S(2)}) copy-start(f32[768]{0:T(1024)S(1)} %reshape.273) | copy-start | bytes 9220
  294.0 5.1 copy-start.41
  299.1 2.2 copy-start.4
  322.0 84.5 %reduce-scatter.33.cloned.1.call-start = ((), (), s32[]{:S(2)}) async-start(), calls=%async_computation.20 | async-start | bytes 3538944
  331.6 92.5 %reduce-scatter.29.cloned.1.call-start = ((), (), s32[]{:S(2)}) async-start(), calls=%async_computation.18 | async-start | bytes 884736
  331.6 6.0 copy-start.49
  331.6 6.0 copy-start.51
  337.6 3.1 copy-start.17
  342.5 18.0 %copy-start.10 = (bf16[384,768]{1,0:T(8,128)(2,1)S(1)}, bf16[384,768]{1,0:T(8,128)(2,1)}, u32[]{:S(2)}) copy-start(bf16[384,768]{1,0:T(8,128)(2,1)} %copy-done.9) | copy-start | bytes 1769476
  342.5 93.6 %reduce-scatter.27.cloned.1.call-start = ((), (), s32[]{:S(2)}) async-start(), calls=%async_computation.17 | async-start | bytes 24576
  342.5 17.9 %copy-start.11 = (f32[2,384,768]{2,1,0:T(8,128)S(1)}, f32[2,384,768]{2,1,0:T(8,128)}, u32[]{:S(2)}) copy-start(f32[2,384,768]{2,1,0:T(8,128)} %fusion.43) | copy-start | bytes 7077892
  358.6 1.0 copy-start.6
  362.3 3.0 copy-start.23
  365.1 0.7 copy-start.28
  365.1 1.8 copy-start.12
  373.5 160.7 %all-reduce.14.cloned.1.call-start = ((), (), s32[]{:S(2)}) async-start(), calls=%async_computation.22 | async-start | bytes 7077888 | tf_op jit(solution)/shard_map/psum | solution.py:177
  378.0 0.7 copy-start.27
  378.0 0.7 copy-start.33
  378.0 0.7 copy-start.42
  378.0 193.9 %reduce-scatter.23.cloned.1.call-start = ((), (), s32[]{:S(2)}) async-start(), calls=%async_computation.15 | async-start | bytes 3538944 | tf_op jit(solution)/shard_map/reduce_scatter | solution.py:311
  384.1 218.8 %reduce-scatter.21.cloned.1.call-start = ((), (), s32[]{:S(2)}) async-start(), calls=%async_computation.14 | async-start | bytes 2654208 | tf_op jit(solution)/shard_map/reduce_scatter | solution.py:293
  389.0 0.9 copy-start.47
  389.0 5.9 copy-start.48
  389.0 10.8 %copy-start.50 = (u32[32]{0:T(128)S(1)}, u32[32]{0:T(128)}, u32[]{:S(2)}) copy-start(u32[32]{0:T(128)} %constant.140) | copy-start | bytes 388
  389.0 303.0 %all-reduce.12.cloned.1.call-start = ((), (), s32[]{:S(2)}) async-start(), calls=%async_computation.21 | async-start | bytes 7077888 | tf_op jit(solution)/shard_map/psum | solution.py:275
  534.3 4.3 copy-start.1
  534.3 4.3 copy-start.2
  536.5 3.7 copy-start.30
  602.9 60.1 %copy-start.34 = (f32[2,384]{1,0:T(2,128)S(1)}, f32[2,384]{1,0:T(2,128)}, u32[]{:S(2)}) copy-start(f32[2,384]{1,0:T(2,128)} %copy-done.31) | copy-start | bytes 9220
  692.0 3.1 copy-start.13
  695.1 1.6 copy-start.14
  695.1 2.9 copy-start.19
  696.6 2.2 copy-start.37
  (3 other events, 1.9 us)
Sparse Core Ops, SparseCore 0:
  10.2 32.4 all-gather.13
  49.9 51.4 all-gather.15
  103.6 50.2 all-gather.21
  155.3 34.7 all-gather.17
  191.5 36.0 all-gather.19
  248.8 54.6 reduce-scatter.24
  305.8 53.3 reduce-scatter.18
  361.3 8.1 reduce-scatter.30
  371.8 34.7 reduce-scatter.32
  408.8 15.2 reduce-scatter.28
  426.3 9.7 reduce-scatter.26
  439.5 94.7 all-reduce.13
  537.2 34.6 reduce-scatter.22
  574.6 28.2 reduce-scatter.20
  606.1 85.8 all-reduce.11
where the time goes:
time: 712 us; the launch traced here: 706 us
  waiting for transfers between devices  269 us (38%)
  matrix products  189 us (27%)
  blocking collectives  83.7 us (12%)
  other arithmetic  77.9 us (11%)
  local copies, waits for them, and re-layouts  71.1 us (10%)
  between operations  15.5 us (2%)
    psum x1, waiting for transfers between devices, per_device(): lax.psum(partial_terms.astype(jnp.bfloat16), 'tensor').astype(jnp.float32)  96.7 us
    unnamed x133, local copies, waits for them, and re-layouts  55.7 us
    dot_general x1, matrix products, per_device(): jnp.einsum('sqhd,skhd->shqk', grad_heads4, value_heads, preferred_element...  34.7 us
    all_gather x1, waiting for transfers between devices, per_device(): key_piece = lax.all_gather(keys_bf, 'context', axis=1, tiled=True)  34.4 us
    reduce_scatter x1, waiting for transfers between devices, per_device(): lax.psum_scatter(summed[8].astype(jnp.bfloat16), 'fsdp', scatter_dimensio...  31.1 us
    reduce_scatter x1, waiting for transfers between devices, per_device(): lax.psum_scatter(summed[2].astype(jnp.bfloat16), 'fsdp', scatter_dimensio...  31 us
    unnamed x20, waiting for transfers between devices  30.4 us
    psum x1, blocking collectives, per_device(): lax.psum(first_gain_grad.astype(jnp.bfloat16), 'context')  30 us
  transfers between devices with their start and end apart: 15, of which 10 were waited for; matrix products, arithmetic and copies ran while one was open for 44% of the time, Pallas kernels for 0%

commit v1 on v0

v1 whole, which is shorter than its diff:
```python
import math

import jax
import jax.numpy as jnp
from jax import lax
from jax.experimental import pallas as pl
from jax.experimental.pallas import tpu as pltpu
from jax.sharding import PartitionSpec as P

HEAD_SIZE = 64
ROT = 16
PAIR = 2 * HEAD_SIZE


norm_eps = 1e-05
rotary_base = 10000.0
masked_score = -1e30


def dot(a, b, ca, cb):
    return lax.dot_general(a, b, (((ca,), (cb,)), ((), ())), preferred_element_type=jnp.float32)


def attention_kernel(
    members, half, q_ref, do_ref, kv_ref, o_ref, dq_ref, dkv_ref,
    qs, dos, scores, probs, offsets, top, total, acc, dkv
):
    both = 2 * half
    blocks = members // 2
    member = lax.axis_index("context")
    lane = lax.broadcasted_iota(jnp.int32, (half, PAIR), 1)
    first = lane < HEAD_SIZE
    zero = jnp.zeros((half, PAIR), jnp.bfloat16)
    for side in range(2):
        q = q_ref[0, side * half:(side + 1) * half, :]
        g = do_ref[0, side * half:(side + 1) * half, :]
        qs[side, 0:half, :] = jnp.where(first, q, zero)
        qs[side, half:both, :] = jnp.where(first, zero, q)
        dos[side, 0:half, :] = jnp.where(first, g, zero)
        dos[side, half:both, :] = jnp.where(first, zero, g)
    row = lax.broadcasted_iota(jnp.int32, (both, both), 0)
    column = lax.broadcasted_iota(jnp.int32, (both, both), 1)
    offsets[...] = row - jnp.where(column >= half, column - half, column)
    top[...] = jnp.full(top.shape, masked_score, jnp.float32)
    total[...] = jnp.zeros(total.shape, jnp.float32)
    acc[...] = jnp.zeros(acc.shape, jnp.float32)
    dkv[...] = jnp.zeros(dkv.shape, jnp.float32)

    low_jobs = (member + 2) // 2
    jobs = 2 * blocks + 1

    def partial_job(t):
        low = t < low_jobs
        block = jnp.where(low, t, t - low_jobs)
        side = jnp.where(low, 0, 1)
        query_base = jnp.where(low, member, 2 * members - 1 - member) * half
        key_base = jnp.where(low, 0, members * half) + block * both
        first_member = jnp.where(low, 2 * block, members - 1 - 2 * block)
        second_member = jnp.where(low, 2 * block + 1, members - 2 - 2 * block)
        return side, side, first_member, second_member, query_base - key_base

    def load(which, part, a, b):
        return jnp.concatenate([kv_ref[a, which, 0, part], kv_ref[b, which, 0, part]], axis=0)

    def score_job(t, side, part, a, b, limit):
        s = dot(load(0, part, a, b), qs[side], 1, 1)
        if limit is not None:
            s = jnp.where(offsets[...] <= limit, s, masked_score)
        scores[t] = s
        top[side] = jnp.maximum(top[side], jnp.max(s, axis=0, keepdims=True))

    def prob_job(t, side, part, a, b):
        p = jnp.exp(scores[t] - top[side])
        total[side] += jnp.sum(p, axis=0, keepdims=True)
        p = p.astype(jnp.bfloat16)
        probs[t] = p
        acc[side] += dot(load(1, part, a, b), p, 0, 0)

    def back_job(t, side, part, a, b):
        p = probs[t]
        k = load(0, part, a, b)
        dp = dot(load(1, part, a, b), dos[side], 1, 1)
        ds = (p.astype(jnp.float32) * (dp - total[side])).astype(jnp.bfloat16)
        acc[side] += dot(k, ds, 0, 0)
        dk = dot(ds, qs[side], 1, 0)
        dv = dot(p, dos[side], 1, 0)
        dkv[a, 0, part] += dk[:half]
        dkv[b, 0, part] += dk[half:]
        dkv[a, 1, part] += dv[:half]
        dkv[b, 1, part] += dv[half:]

    def run(job, masked):
        @pl.loop(0, blocks)
        def _(t):
            job(t, 1, 0, 2 * t, 2 * t + 1, *((None,) if masked else ()))

        @pl.loop(0, blocks + 1)
        def _(t):
            side, part, a, b, limit = partial_job(t)
            job(t + blocks, side, part, a, b, *((limit,) if masked else ()))

    run(score_job, True)
    run(prob_job, False)
    for side in range(2):
        inverse = 1.0 / total[side]
        o = acc[side] * inverse
        g = jnp.transpose(dos[side].astype(jnp.float32))
        total[side] = jnp.sum(o * g, axis=0, keepdims=True) * inverse
        dos[side] = jnp.transpose(g * inverse).astype(jnp.bfloat16)
        o = jnp.transpose(o)
        o_ref[0, side * half:(side + 1) * half, :] = jnp.where(
            first, o[:half], o[half:]).astype(o_ref.dtype)
    acc[...] = jnp.zeros(acc.shape, jnp.float32)
    run(back_job, False)
    for side in range(2):
        dq = jnp.transpose(acc[side] * (1.0 / math.sqrt(HEAD_SIZE)))
        dq_ref[0, side * half:(side + 1) * half, :] = jnp.where(
            first, dq[:half], dq[half:]).astype(dq_ref.dtype)
    dkv_ref[:, :, 0] = dkv[...].astype(dkv_ref.dtype)


def attention(queries, grads, keys_values):
    seqs, rows, width = queries.shape
    members = keys_values.shape[0]
    half = rows // 2
    both = 2 * half
    keys_values = keys_values.reshape(members, 2, seqs, 2, half, width)
    row_spec = pl.BlockSpec((1, rows, PAIR), lambda s, p: (s, 0, p))
    kv_spec = pl.BlockSpec((members, 2, 1, 2, half, PAIR), lambda s, p: (0, 0, s, 0, 0, p))
    jobs = members + 1
    work = seqs * (width // PAIR) * jobs * both * both * PAIR * 2
    out = pl.pallas_call(
        lambda *refs: attention_kernel(members, half, *refs),
        grid=(seqs, width // PAIR),
        in_specs=[row_spec, row_spec, kv_spec],
        out_specs=[row_spec, row_spec, kv_spec],
        out_shape=[
            jax.ShapeDtypeStruct(queries.shape, jnp.bfloat16),
            jax.ShapeDtypeStruct(queries.shape, jnp.float32),
            jax.ShapeDtypeStruct(keys_values.shape, jnp.bfloat16),
        ],
        scratch_shapes=[
            pltpu.VMEM((2, both, PAIR), jnp.bfloat16),
            pltpu.VMEM((2, both, PAIR), jnp.bfloat16),
            pltpu.VMEM((jobs, both, both), jnp.float32),
            pltpu.VMEM((jobs, both, both), jnp.bfloat16),
            pltpu.VMEM((both, both), jnp.int32),
            pltpu.VMEM((2, 1, both), jnp.float32),
            pltpu.VMEM((2, 1, both), jnp.float32),
            pltpu.VMEM((2, PAIR, both), jnp.float32),
            pltpu.VMEM((members, 2, 2, half, PAIR), jnp.float32),
        ],
        compiler_params=pltpu.CompilerParams(vmem_limit_bytes=50 * 1024 * 1024),
        cost_estimate=pl.CostEstimate(
            flops=work * 6,
            bytes_accessed=2 * 2 * keys_values.size + 8 * queries.size,
            transcendentals=seqs * (width // PAIR) * jobs * both * both,
        ),
    )(queries, grads, keys_values)
    return out[0], out[1], out[2].reshape(members, 2, seqs, rows, width)


def rotate(values, cosine, sine_table):
    half_dim = ROT // 2
    leading = values[..., :half_dim]
    trailing = values[..., half_dim:ROT]
    return jnp.concatenate(
        [
            leading * cosine - trailing * sine_table,
            trailing * cosine + leading * sine_table,
            values[..., ROT:],
        ],
        axis=-1,
    )


def arranged_position(member, within, block_rows, members):
    half_rows = block_rows // 2
    return jnp.where(
        within < half_rows,
        member * half_rows + within,
        (2 * members - 1 - member) * half_rows + within - half_rows,
    )


def mm(a, b, ca, cb):
    return lax.dot_general(a, b, (((ca,), (cb,)), ((), ())), preferred_element_type=jnp.float32)


def per_device(
    layer_input,
    attention_gain,
    attention_shift,
    query_key_value_weight,
    query_key_value_bias,
    attention_output_weight,
    output_bias,
    feed_gain,
    feed_shift,
    up_projection_weight,
    up_projection_bias,
    down_projection_weight,
    down_bias,
    cotangent,
):
    f32, bf16 = jnp.float32, jnp.bfloat16
    seqs, rows, model = layer_input.shape
    tokens = seqs * rows
    parts = lax.axis_size("fsdp")
    members = lax.axis_size("context")
    member = lax.axis_index("context")
    share = model // parts
    width = query_key_value_weight.shape[2]
    heads = width // HEAD_SIZE
    hidden_width = up_projection_weight.shape[1]

    small = [
        attention_gain, attention_shift, query_key_value_bias, output_bias,
        feed_gain, feed_shift, up_projection_bias, down_bias,
    ]
    packed = lax.all_gather(jnp.concatenate([v.reshape(-1) for v in small]), "fsdp", axis=0)
    whole = []
    start = 0
    for v in small:
        piece = packed[:, start:start + v.size].astype(f32).reshape((parts,) + v.shape)
        start += v.size
        whole.append(jnp.moveaxis(piece, 0, -2).reshape(v.shape[:-1] + (parts * v.shape[-1],)))
    gain_a, shift_a, heads_bias, bias_o, gain_f, shift_f, up_bias, bias_d = whole
    heads_weight = lax.all_gather(query_key_value_weight, "fsdp", axis=0, tiled=True)
    heads_weight = heads_weight.reshape(model, 3 * width)
    up_weight = lax.all_gather(up_projection_weight, "fsdp", axis=0, tiled=True)
    down_weight = lax.all_gather(down_projection_weight, "fsdp", axis=1, tiled=True)
    output_weight = lax.all_gather(attention_output_weight, "fsdp", axis=1, tiled=True)

    place = arranged_position(member, jnp.arange(rows, dtype=jnp.int32), rows, members)
    frequency = jnp.power(
        jnp.float32(rotary_base), -2.0 * jnp.arange(ROT // 2, dtype=f32) / ROT
    )
    phases = place.astype(f32)[:, None] * frequency[None, :]
    cosine = jnp.cos(phases)[:, None, :]
    sine = jnp.sin(phases)[:, None, :]

    x = layer_input.astype(f32).reshape(tokens, model)
    dy_bf = cotangent.reshape(tokens, model)
    dy = dy_bf.astype(f32)
    center = x - jnp.mean(x, axis=-1, keepdims=True)
    scale = lax.rsqrt(jnp.mean(center * center, axis=-1, keepdims=True) + norm_eps)
    xhat = center * scale
    normed_a = (xhat * gain_a + shift_a).astype(bf16)
    normed_f = (xhat * gain_f + shift_f).astype(bf16)

    projected = mm(normed_a, heads_weight, 1, 0) + heads_bias.reshape(-1)
    projected = projected.reshape(seqs, rows, 3, width)
    head_shape = (seqs, rows, heads, HEAD_SIZE)
    queries = rotate(projected[:, :, 0].reshape(head_shape), cosine, sine).astype(bf16)
    keys = rotate(projected[:, :, 1].reshape(head_shape), cosine, sine).astype(bf16)
    flat = (seqs, rows, width)
    keys_values = jnp.stack([keys.reshape(flat), projected[:, :, 2].astype(bf16)])
    keys_values = lax.all_gather(keys_values, "context", axis=0)
    queries = queries.reshape(flat) * jnp.bfloat16(1.0 / math.sqrt(HEAD_SIZE))

    hidden = mm(normed_f, up_weight, 1, 0) + up_bias.reshape(-1)
    gelu_output, gelu_back = jax.vjp(lambda t: jax.nn.gelu(t, approximate=False), hidden)
    activated = gelu_output.astype(bf16)
    feed_terms = mm(activated, down_weight, 1, 0)
    hidden_grad = gelu_back(mm(dy_bf, down_weight, 1, 1))[0].astype(bf16)
    down_grad = mm(activated, dy_bf, 0, 0)
    up_grad = mm(normed_f, hidden_grad, 0, 0)
    up_bias_grad = jnp.sum(hidden_grad.astype(f32), axis=0)
    feed_part = mm(hidden_grad, up_weight, 1, 1)

    attended_grad = mm(dy_bf, output_weight, 1, 1).astype(bf16).reshape(flat)
    attended, query_grad, kv_grad = attention(queries, attended_grad, keys_values)
    own = lax.psum_scatter(kv_grad, "context", scatter_dimension=0, tiled=True)[0]

    attended = attended.reshape(tokens, width)
    terms = mm(attended, output_weight, 1, 0) + feed_terms
    branches = lax.psum(terms.astype(bf16), "tensor").astype(f32)
    layer_output = (x + branches + bias_o + bias_d).astype(bf16)
    output_grad = mm(attended, dy_bf, 0, 0)

    query_back = rotate(query_grad.reshape(head_shape), cosine, -sine)
    key_back = rotate(own[0].astype(f32).reshape(head_shape), cosine, -sine)
    projected_grad = jnp.concatenate(
        [query_back.reshape(flat).astype(bf16), key_back.reshape(flat).astype(bf16), own[1]],
        axis=-1,
    ).reshape(tokens, 3 * width)
    heads_grad = mm(normed_a, projected_grad, 0, 0)
    heads_bias_grad = jnp.sum(projected_grad.astype(f32), axis=0)
    heads_part = mm(projected_grad, heads_weight, 1, 1)

    combined = lax.psum((heads_part * gain_a + feed_part * gain_f).astype(bf16), "tensor")
    combined = combined.astype(f32)
    input_grad = dy + scale * (
        combined
        - jnp.mean(combined, axis=-1, keepdims=True)
        - xhat * jnp.mean(combined * xhat, axis=-1, keepdims=True)
    )

    def reduce_columns(grad):
        grad = lax.psum_scatter(grad.astype(bf16), "fsdp", scatter_dimension=1, tiled=True)
        return lax.psum(grad, "context").astype(f32)

    def reduce_rows(grad):
        grad = lax.psum_scatter(grad.astype(bf16), "fsdp", scatter_dimension=0, tiled=True)
        return lax.psum(grad, "context").astype(f32)

    up_out = reduce_rows(up_grad)
    down_out = reduce_columns(down_grad)
    output_out = reduce_columns(output_grad)
    heads_out = reduce_rows(heads_grad).reshape(share, 3, width)

    def by_part(v):
        v = v.reshape(v.shape[:-1] + (parts, v.shape[-1] // parts))
        return jnp.moveaxis(v, -2, 0).reshape(parts, -1)

    shared = jnp.concatenate([by_part(v) for v in (
        jnp.sum(heads_part * xhat, axis=0), jnp.sum(heads_part, axis=0),
        jnp.sum(feed_part * xhat, axis=0), jnp.sum(feed_part, axis=0))], axis=1)
    single = jnp.concatenate([by_part(v) for v in (
        jnp.sum(dy, axis=0), heads_bias_grad.reshape(3, heads, HEAD_SIZE),
        up_bias_grad.reshape(-1, HEAD_SIZE))], axis=1)
    shared = lax.psum(shared, "tensor")
    vectors = lax.psum_scatter(
        jnp.concatenate([shared, single], axis=1), "fsdp", scatter_dimension=0, tiled=True)
    vectors = lax.psum(vectors, "context")[0]
    sizes = [share] * 5 + [3 * heads * HEAD_SIZE // parts, hidden_width // parts]
    pieces = []
    start = 0
    for size in sizes:
        pieces.append(vectors[start:start + size])
        start += size
    return (
        layer_output.reshape(seqs, rows, model),
        input_grad.reshape(seqs, rows, model),
        pieces[0],
        pieces[1],
        heads_out,
        pieces[5].reshape(query_key_value_bias.shape),
        output_out,
        pieces[4],
        pieces[2],
        pieces[3],
        up_out,
        pieces[6].reshape(up_projection_bias.shape),
        down_out,
        pieces[4],
    )


def solution(mesh):
    in_specs = (
        P("fsdp", "context", None),
        P("fsdp"),
        P("fsdp"),
        P("fsdp", None, "tensor"),
        P(None, "tensor", "fsdp"),
        P("tensor", "fsdp"),
        P("fsdp"),
        P("fsdp"),
        P("fsdp"),
        P("fsdp", "tensor"),
        P("tensor", "fsdp"),
        P("tensor", "fsdp"),
        P("fsdp"),
        P("fsdp", "context", None),
    )
    out_specs = (
        P("fsdp", "context", None),
        P("fsdp", "context", None),
        P("fsdp"),
        P("fsdp"),
        P("fsdp", None, "tensor"),
        P(None, "tensor", "fsdp"),
        P("tensor", "fsdp"),
        P("fsdp"),
        P("fsdp"),
        P("fsdp"),
        P("fsdp", "tensor"),
        P("tensor", "fsdp"),
        P("tensor", "fsdp"),
        P("fsdp"),
    )
    return jax.shard_map(
        per_device, mesh=mesh, in_specs=in_specs, out_specs=out_specs, check_vma=False
    )
```

time: 712 us -> 656 us (0.921)
  matrix products: 189 us -> 56.3 us
  waiting for transfers between devices: 269 us -> 347 us
  Pallas kernels: 0 us -> 71.1 us
  other arithmetic: 77.9 us -> 24.2 us
  blocking collectives: 83.7 us -> 62.6 us
    dot_general x18 -> x12, matrix products: 189 us -> 56.3 us  [mm(): lax.dot_general(a, b, (((ca,), (cb,)), ((), ())), preferred_element_type=...]
    pallas_call x0 -> x1, Pallas kernels: none -> 71.1 us  [attention(): pl.pallas_call(lambda *refs: attention_kernel(members, half, *refs), grid...]
    reduce_scatter x3, waiting for transfers between devices: 62.1 us -> 115 us  [the longest x2 64.1 us: reduce_rows(): lax.psum_scatter(grad.astype(bf16), 'fsdp', scatter_dimension=0, tiled=True)]
    all_gather x3 -> x2, waiting for transfers between devices: 38.4 us -> 78.8 us  [the longest x1 78.8 us: per_device(): keys_values = lax.all_gather(keys_values, 'context', axis=0)]
    all_gather x8 -> x0, blocking collectives: 36.1 us -> none  [the longest x1 5.22 us: per_device(): lax.all_gather(attention_gain, 'fsdp', axis=0, tiled=True)]
    unnamed x133 -> x104, local copies, waits for them, and re-layouts: 55.7 us -> 21.9 us
    reduce_sum x10 -> x5, other arithmetic: 35.5 us -> 5.07 us  [the longest x1 3.84 us: per_device(): jnp.sum(heads_part * xhat, axis=0)]
    psum x2, waiting for transfers between devices: 121 us -> 94.4 us  [the longest x1 54.5 us: per_device(): branches = lax.psum(terms.astype(bf16), 'tensor').astype(f32)]
  transfers between devices with their start and end apart: 15 -> 11, of which waited for: 10 -> 9; matrix products, arithmetic and copies ran while one was open for 44% -> 16% of each run, Pallas kernels for 0% -> 11%
where the time goes in v1:
time: 656 us; the launch traced here: 647 us
  waiting for transfers between devices  347 us (53%)
  Pallas kernels  71.1 us (11%)
  local copies, waits for them, and re-layouts  69.7 us (11%)
  blocking collectives  62.6 us (10%)
  matrix products  56.3 us (9%)
  other arithmetic  24.2 us (4%)
  between operations  15.7 us (2%)
    all_gather x1, waiting for transfers between devices, per_device(): keys_values = lax.all_gather(keys_values, 'context', axis=0)  78.8 us
    pallas_call x1, Pallas kernels, attention(): pl.pallas_call(lambda *refs: attention_kernel(members, half, *refs), grid...  71.1 us
    reduce_scatter x2, waiting for transfers between devices, reduce_rows(): lax.psum_scatter(grad.astype(bf16), 'fsdp', scatter_dimension=0, tiled=True)  64.1 us
    dot_general x12, matrix products, mm(): lax.dot_general(a, b, (((ca,), (cb,)), ((), ())), preferred_element_type=...  56.3 us
    psum x1, waiting for transfers between devices, per_device(): branches = lax.psum(terms.astype(bf16), 'tensor').astype(f32)  54.5 us
    reduce_scatter x1, waiting for transfers between devices, per_device(): lax.psum_scatter(kv_grad, 'context', scatter_dimension=0, tiled=True)[0]  51.3 us
    unnamed x13, waiting for transfers between devices  40.3 us
    psum x1, waiting for transfers between devices, reduce_rows(): return lax.psum(grad, 'context').astype(f32)  39.9 us
  transfers between devices with their start and end apart: 11, of which 9 were waited for; matrix products, arithmetic and copies ran while one was open for 16% of the time, Pallas kernels for 11%

profile of v1, /device:TPU:0, one launch (start us, length us, event | category | flops | bytes accessed | tf_op | source)
XLA Modules:
  0.0 647.3 jit_solution(3822115944350318160)
XLA Ops:
  7.3 2.4 copy.67
  11.7 9.6 %all-reduce = bf16[7296]{0:T(1024)(128)(2,1)S(1)} all-reduce(bf16[7296]{0:T(1024)(128)(2,1)S(1)} %dynamic-update-slice), channel_id=2, replica_groups=mesh['fsdp'=2,'context'=8,'tensor'=2] {'fsdp'}, use_global_device_ids=true, to_apply=%add | all-reduce | flops 7296 | bytes 29184
  21.4 0.7 slice_convert_fusion.7
  23.1 0.7 fusion.33
  24.4 18.0 %all-gather.7.cloned.1.call-done = bf16[768,3,384]{0,2,1:T(8,128)(2,1)} async-done(((bf16[384,3,384]{0,2,1:T(8,128)(2,1)}), bf16[768,3,384]{0,2,1:T(8,128)(2,1)}) %all-gather.7.cloned.1.call-update) | async-done | bytes 1769488 | tf_op jit(solution)/shard_map/all_gather | solution.py:229
  42.4 5.0 convolution_add_fusion
  47.4 3.3 copy.69
  50.7 3.4 reshape.336
  54.0 2.4 fusion.35
  56.5 1.7 fusion.32
  59.8 1.7 pad_maximum_fusion
  61.5 3.2 copy.73
  64.8 0.7 all-gather.9.cloned.1.call-update
  66.1 9.6 %all_gather.27 = bf16[384,768]{1,0:T(8,128)(2,1)S(1)} all-gather(bf16[384,384]{1,0:T(8,128)(2,1)S(1)} %copy-done.13), channel_id=1, replica_groups=mesh['fsdp'=2,'context'=8,'tensor'=2] {'fsdp'}, dimensions={1}, use_global_device_ids=true | all-gather | bytes 884736 | tf_op jit(solution)/shard_map/all_gather | solution.py:233
  75.7 0.8 convolution_convert_fusion.3
  76.9 78.8 %all-gather.13.cloned.1.call-done = bf16[16,2,384,384]{3,2,1,0:T(8,128)(2,1)} async-done(((bf16[2,2,384,384]{3,2,1,0:T(8,128)(2,1)}), bf16[16,2,384,384]{3,2,1,0:T(8,128)(2,1)}) %all-gather.13.cloned.1.call-update) | async-done | bytes 9437200 | tf_op jit(solution)/shard_map/all_gather | solution.py:259
  155.7 71.1 %shard_map.245 = (bf16[2,384,384]{2,1,0:T(8,128)(2,1)S(1)}, f32[2,384,384]{2,1,0:T(8,128)S(1)}, bf16[8,2,2,2,192,384]{5,4,3,2,1,0:T(8,128)(2,1)}) custom-call(bf16[2,384,384]{2,1,0:T(8,128)(2,1)S(1)} %copy.74.refs_0_, bf16[2,384,384]{2,1,0:T(8,128)(2,1)S(1)} %bitcast.112, bf16[8,2,2,2,192,384]{5,4,3,2,1,0:T(8,128)(2,1)} %bitcast.145), custom_call_target="tpu_custom_call" | custom-call | flops 12230590464 | bytes 21233664 | tf_op jit(solution)/shard_map/pallas_call | solution.py:132
  226.8 12.7 %copy.78 = bf16[8,2,2,384,384]{3,4,2,1,0:T(8,128)(2,1)} copy(bf16[8,2,2,384,384]{4,3,2,1,0:T(8,128)(2,1)} %bitcast.113) | data formatting | bytes 18874368 | tf_op jit(solution)/shard_map/reshape | solution.py:160
  239.6 0.8 rsqrt.13
  240.4 1.3 div.23
  241.6 1.3 reshape.360
  242.9 1.3 reshape.361
  244.2 1.4 slice_convert_fusion.4
  245.6 1.4 reshape.366
  246.9 1.4 copy.75
  248.3 1.4 reshape.362
  249.7 2.2 fusion.23
  251.9 6.3 fusion.38
  258.2 16.9 %convert_reduce_fusion = (f32[1536]{0:T(1024)}, bf16[768,1536]{1,0:T(8,128)(2,1)}, f32[768,1536]{1,0:T(8,128)S(1)}) fusion(f32[768,1536]{1,0:T(8,128)} %fusion.38, f32[1536]{0:T(1024)} %reshape.362, bf16[768,768]{1,0:T(8,128)(2,1)} %bitcast.115, bf16[1536,768]{1,0:T(8,128)(2,1)} %all-gather.11.cloned.1.call-done), kind=kOutput, calls=%fused_computation.2 | convolution fusion | flops 1900411392 | bytes 15347712 | tf_op jit(solution)/shard_map/dot_general | solution.py:187
  275.1 1.2 multiply_convert_fusion
  276.8 3.4 fusion.39
  280.2 1.4 copy.76
  281.6 1.2 slice.226
  282.8 3.6 add_convert_fusion.2
  286.4 51.3 %reduce-scatter.10.cloned.1.call-done = bf16[1,2,2,384,384]{3,4,2,1,0:T(8,128)(2,1)} async-done(((bf16[8,2,2,384,384]{3,4,2,1,0:T(8,128)(2,1)}), bf16[1,2,2,384,384]{3,4,2,1,0:T(8,128)(2,1)}) %reduce-scatter.10.cloned.1.call-update) | async-done | bytes 1179664 | tf_op jit(solution)/shard_map/reduce_scatter | solution.py:274
  337.7 1.4 fusion.36
  339.2 1.1 subtract_convert_fusion
  343.4 1.8 fusion.40
  345.7 1.3 copy-done.43
  347.0 3.8 add_convert_fusion.1
  350.9 1.2 copy-done.4
  352.1 5.1 convolution_convert_fusion
  357.2 4.3 copy.89
  362.5 1.1 copy.87
  363.6 54.5 %all-reduce.9.cloned.1.call-done = (bf16[768,768]{1,0:T(8,128)(2,1)}, bf16[768,768]{1,0:T(8,128)(2,1)}) async-done(((bf16[768,768]{1,0:T(8,128)(2,1)}, bf16[768,768]{1,0:T(8,128)(2,1)}), (bf16[768,768]{1,0:T(8,128)(2,1)}, bf16[768,768]{1,0:T(8,128)(2,1)})) %all-reduce.9.cloned.1.call-update) | async-done | bytes 2359312 | tf_op jit(solution)/shard_map/psum | solution.py:278
  418.1 3.8 fusion.24
  422.0 3.0 convolution_convert_fusion.2
  425.0 6.1 convolution_convert_fusion.1
  432.0 23.2 %reduce-scatter.18.cloned.1.call-done = bf16[384,1536]{1,0:T(8,128)(2,1)} async-done(((bf16[768,1536]{1,0:T(8,128)(2,1)}), bf16[384,1536]{1,0:T(8,128)(2,1)}) %reduce-scatter.18.cloned.1.call-update) | async-done | bytes 1179664
  455.2 2.4 copy.90
  457.6 15.8 %reduce-scatter.16.cloned.1.call-done = bf16[384,384]{1,0:T(8,128)(2,1)} async-done(((bf16[768,384]{1,0:T(8,128)(2,1)}), bf16[384,384]{1,0:T(8,128)(2,1)}) %reduce-scatter.16.cloned.1.call-update) | async-done | bytes 294928
  473.3 1.8 copy.88
  475.7 28.8 %reduce-scatter.12.cloned.1.call-done = bf16[384,1152]{1,0:T(8,128)(2,1)} async-done(((bf16[768,1152]{1,0:T(8,128)(2,1)}), bf16[384,1152]{1,0:T(8,128)(2,1)}) %reduce-scatter.12.cloned.1.call-update) | async-done | bytes 884752 | tf_op jit(solution)/shard_map/reduce_scatter | solution.py:305
  504.6 2.2 copy.83
  506.8 35.2 %reduce-scatter.14.cloned.1.call-done = bf16[384,1536]{1,0:T(8,128)(2,1)} async-done(((bf16[768,1536]{1,0:T(8,128)(2,1)}), bf16[384,1536]{1,0:T(8,128)(2,1)}) %reduce-scatter.14.cloned.1.call-update) | async-done | bytes 1179664 | tf_op jit(solution)/shard_map/reduce_scatter | solution.py:305
  542.0 8.1 %psum.58 = f32[2,1536]{1,0:T(2,128)S(1)} all-reduce(f32[2,1536]{1,0:T(2,128)S(1)} %pad_maximum_fusion.4), channel_id=1, replica_groups=mesh['fsdp'=2,'context'=8,'tensor'=2] {'tensor'}, use_global_device_ids=true, to_apply=%region_11.12 | all-reduce | flops 3072 | bytes 24576 | tf_op jit(solution)/shard_map/psum | solution.py:323
  550.2 7.4 %all-reduce.1 = f32[2,3264]{1,0:T(2,128)S(1)} all-reduce(f32[2,3264]{1,0:T(2,128)S(1)} %concatenate.39), channel_id=5, replica_groups=mesh['fsdp'=2,'context'=8,'tensor'=2] {'fsdp'}, use_global_device_ids=true, to_apply=%region_15.16.clone | all-reduce | flops 6528 | bytes 52224
  558.3 28.0 %psum.59 = f32[1,3264]{1,0:T(1,128)S(1)} all-reduce(f32[1,3264]{1,0:T(1,128)S(1)} %constant_dynamic-slice_fusion), channel_id=1, replica_groups=mesh['fsdp'=2,'context'=8,'tensor'=2] {'context'}, use_global_device_ids=true, to_apply=%region_16.17 | all-reduce | flops 3264 | bytes 26112 | tf_op jit(solution)/shard_map/psum | solution.py:326
  588.3 3.7 fusion.8
  592.0 39.9 %all-reduce.7.cloned.1.call-done = (bf16[384,3,384]{0,2,1:T(8,128)(2,1)}, bf16[384,384]{1,0:T(8,128)(2,1)}, bf16[384,1536]{1,0:T(8,128)(2,1)}, bf16[1536,384]{1,0:T(8,128)(2,1)}) async-done(((bf16[384,3,384]{0,2,1:T(8,128)(2,1)}, bf16[384,384]{1,0:T(8,128)(2,1)}, bf16[384,1536]{1,0:T(8,128)(2,1)}, bf16[1536,384]{1,0:T(8,128)(2,1)}), (bf16[384,3,384]{0,2,1:T(8,128)(2,1)}, bf16[384,384]{1,0:T(8,128)(2,1)}, ...) | async-done | bytes 3538960 | tf_op jit(solution)/shard_map/psum | solution.py:306
  631.9 3.1 convert_element_type.157
  635.0 1.6 convert_element_type.159
  636.5 2.4 copy.85
  638.9 0.9 convert_element_type.155
  (177 shorter events, 15.6 us)
Async XLA Ops:
  7.2 2.8 copy-start.33
  7.2 2.6 copy-start.31
  7.2 2.7 copy-start.32
  7.2 4.0 copy-start.34
  7.2 4.0 copy-start.35
  7.2 4.0 copy-start.36
  7.2 4.0 copy-start.37
  7.3 4.0 copy-start.38
  7.3 4.0 copy-start.39
  7.3 15.1 %copy-start = (bf16[2,384,768]{2,1,0:T(8,128)(2,1)S(1)}, bf16[2,384,768]{2,1,0:T(8,128)(2,1)}, u32[]{:S(2)}) copy-start(bf16[2,384,768]{2,1,0:T(8,128)(2,1)} %param.14) | copy-start | bytes 3538948
  7.3 35.1 %all-gather.7.cloned.1.call-start = ((), (), s32[]{:S(2)}) async-start(), calls=%async_computation.5 | async-start | bytes 2654208 | tf_op jit(solution)/shard_map/all_gather | solution.py:229
  9.7 145.9 %all-gather.13.cloned.1.call-start = ((), (), s32[]{:S(2)}) async-start(), calls=%async_computation.11 | async-start | bytes 10616832 | tf_op jit(solution)/shard_map/all_gather | solution.py:259
  21.4 0.7 copy-start.16
  22.1 2.3 copy-start.20
  22.2 2.2 copy-start.22
  22.6 19.8 %copy-start.19 = (f32[2,384]{1,0:T(2,128)}, f32[2,384]{1,0:T(2,128)S(1)}, u32[]{:S(2)}) copy-start(f32[2,384]{1,0:T(2,128)S(1)} %broadcast_multiply_fusion.2) | copy-start | bytes 9220
  23.1 19.3 %copy-start.25 = (f32[2,384]{1,0:T(2,128)}, f32[2,384]{1,0:T(2,128)S(1)}, u32[]{:S(2)}) copy-start(f32[2,384]{1,0:T(2,128)S(1)} %add_rsqrt_fusion) | copy-start | bytes 9220
  58.2 0.7 copy-start.18
  64.7 1.4 copy-start.13
  64.7 11.0 %copy-start.3 = (bf16[2,384,768]{2,1,0:T(8,128)(2,1)S(1)}, bf16[2,384,768]{2,1,0:T(8,128)(2,1)}, u32[]{:S(2)}) copy-start(bf16[2,384,768]{2,1,0:T(8,128)(2,1)} %param.27) | copy-start | bytes 3538948
  64.8 187.2 %all-gather.9.cloned.1.call-start = ((), (), s32[]{:S(2)}) async-start(), calls=%async_computation.6 | async-start | bytes 3538944 | tf_op jit(solution)/shard_map/all_gather | solution.py:231
  65.5 192.7 %all-gather.11.cloned.1.call-start = ((), (), s32[]{:S(2)}) async-start(), calls=%async_computation.7 | async-start | bytes 3538944 | tf_op jit(solution)/shard_map/all_gather | solution.py:232
  66.1 271.6 %reduce-scatter.10.cloned.1.call-start = ((), (), s32[]{:S(2)}) async-start(), calls=%async_computation.8 | async-start | bytes 10616832 | tf_op jit(solution)/shard_map/reduce_scatter | solution.py:274
  239.5 10.2 %copy-start.1 = (bf16[2,384,768]{2,1,0:T(8,128)(2,1)S(1)}, bf16[2,384,768]{2,1,0:T(8,128)(2,1)}, u32[]{:S(2)}) copy-start(bf16[2,384,768]{2,1,0:T(8,128)(2,1)} %param.14) | copy-start | bytes 3538948
  239.5 178.6 %all-reduce.9.cloned.1.call-start = ((), (), s32[]{:S(2)}) async-start(), calls=%async_computation.15 | async-start | bytes 4718592 | tf_op jit(solution)/shard_map/psum | solution.py:278
  258.2 16.9 %copy-start.5 = (f32[768,1536]{1,0:T(8,128)S(1)}, f32[768,1536]{1,0:T(8,128)}, u32[]{:S(2)}) copy-start(f32[768,1536]{1,0:T(8,128)} %fusion.38) | copy-start | bytes 14155780
  258.2 16.9 %copy-start.24 = (f32[1536]{0:T(1024)S(1)}, f32[1536]{0:T(1024)}, u32[]{:S(2)}) copy-start(f32[1536]{0:T(1024)} %reshape.362) | copy-start | bytes 18436
  275.1 1.7 copy-start.41
  276.8 3.4 copy-start.9
  286.4 52.8 %copy-start.17 = (f32[384,8]{0,1:T(8,128)S(1)}, f32[384,8]{0,1:T(8,128)}, u32[]{:S(2)}) copy-start(f32[384,8]{0,1:T(8,128)} %get-tuple-element.109) | copy-start | bytes 36868
  341.9 1.5 copy-start.42
  343.4 1.8 copy-start.6
  343.4 1.8 copy-start.21
  343.4 1.8 copy-start.26
  343.4 2.3 copy-start.40
  343.4 3.6 copy-start.43
  345.2 5.6 copy-start.10
  350.8 1.3 copy-start.4
  350.8 104.4 %reduce-scatter.18.cloned.1.call-start = ((), (), s32[]{:S(2)}) async-start(), calls=%async_computation.13 | async-start | bytes 3538944
  361.5 56.6 %copy-start.15 = (f32[768]{0:T(1024)S(1)}, f32[768]{0:T(1024)}, u32[]{:S(2)}) copy-start(f32[768]{0:T(1024)} %div.23) | copy-start | bytes 9220
  361.5 56.6 %copy-start.23 = (f32[768]{0:T(1024)S(1)}, f32[768]{0:T(1024)}, u32[]{:S(2)}) copy-start(f32[768]{0:T(1024)} %copy-done.22) | copy-start | bytes 9220
  361.5 111.8 %reduce-scatter.16.cloned.1.call-start = ((), (), s32[]{:S(2)}) async-start(), calls=%async_computation.12 | async-start | bytes 884736
  363.6 141.0 %reduce-scatter.12.cloned.1.call-start = ((), (), s32[]{:S(2)}) async-start(), calls=%async_computation.9 | async-start | bytes 2654208 | tf_op jit(solution)/shard_map/reduce_scatter | solution.py:305
  418.1 3.8 copy-start.7
  425.0 117.0 %reduce-scatter.14.cloned.1.call-start = ((), (), s32[]{:S(2)}) async-start(), calls=%async_computation.10 | async-start | bytes 3538944 | tf_op jit(solution)/shard_map/reduce_scatter | solution.py:305
  431.1 0.7 copy-start.28
  431.1 0.7 copy-start.27
  431.1 0.7 copy-start.30
  431.1 200.8 %all-reduce.7.cloned.1.call-start = ((), (), s32[]{:S(2)}) async-start(), calls=%async_computation.14 | async-start | bytes 7077888 | tf_op jit(solution)/shard_map/psum | solution.py:306
  431.4 43.8 %copy-start.8 = (bf16[768,1152]{0,1:T(8,128)(2,1)S(1)}, bf16[768,1152]{0,1:T(8,128)(2,1)}, u32[]{:S(2)}) copy-start(bf16[768,1152]{0,1:T(8,128)(2,1)} %copy-done.6) | copy-start | bytes 5308420
  506.8 81.5 %copy-start.2 = (bf16[768,768]{1,0:T(8,128)(2,1)S(1)}, bf16[768,768]{1,0:T(8,128)(2,1)}, u32[]{:S(2)}) copy-start(bf16[768,768]{1,0:T(8,128)(2,1)} %get-tuple-element.80) | copy-start | bytes 3538948
  588.3 51.5 %copy-start.29 = (f32[384]{0:T(512)}, f32[384]{0:T(512)S(1)}, u32[]{:S(2)}) copy-start(f32[384]{0:T(512)S(1)} %get-tuple-element.145) | copy-start | bytes 4612
  631.9 3.1 copy-start.11
  635.0 1.6 copy-start.12
  635.0 3.9 copy-start.14
Sparse Core Ops, SparseCore 0:
  10.2 32.1 all-gather.6
  64.9 90.7 all-gather.12
  157.2 34.5 all-gather.8
  193.2 36.0 all-gather.10
  239.7 97.9 reduce-scatter.9
  351.0 67.1 all-reduce.8
  420.5 34.6 reduce-scatter.17
  458.0 15.2 reduce-scatter.15
  476.3 28.2 reduce-scatter.11
  507.2 34.7 reduce-scatter.13
  546.0 85.8 all-reduce.6

commit v2 on v1

--- a/solution.py
+++ b/solution.py
@@ -160,18 +160,66 @@
     return out[0], out[1], out[2].reshape(members, 2, seqs, rows, width)
 
 
-def rotate(values, cosine, sine_table):
+def rotate(values, even, ahead, behind):
     half_dim = ROT // 2
-    leading = values[..., :half_dim]
-    trailing = values[..., half_dim:ROT]
+    return (
+        values * even
+        + jnp.roll(values, -half_dim, axis=-1) * ahead
+        + jnp.roll(values, half_dim, axis=-1) * behind
+    )
+
+
+def swap(value, axis):
+    return lax.ppermute(value, axis, [(0, 1), (1, 0)])
+
+
+def sibling(value):
+    count = lax.axis_size("context")
+    return lax.ppermute(value, "context", [(i, i ^ 1) for i in range(count)])
+
+
+def whole_weight(shard, axis):
+    if lax.axis_size("fsdp") != 2:
+        return lax.all_gather(shard, "fsdp", axis=axis, tiled=True)
+    core = lax.axis_index("context") % 2
+    rows = shard.shape[0] // 2
+    mine = swap(lax.dynamic_slice_in_dim(shard, core * rows, rows, 0), "fsdp")
+    theirs = sibling(mine)
+    first = jnp.where(core == 0, mine, theirs)
+    second = jnp.where(core == 0, theirs, mine)
+    far = jnp.concatenate([first, second], axis=0)
+    left = lax.axis_index("fsdp") == 0
+    return jnp.concatenate([jnp.where(left, shard, far), jnp.where(left, far, shard)], axis=axis)
+
+
+def sum_pair(value):
+    if lax.axis_size("tensor") != 2:
+        return lax.psum(value, "tensor").astype(jnp.float32)
+    return value.astype(jnp.float32) + swap(value, "tensor").astype(jnp.float32)
+
+
+def reduce_gradient(grad, order):
+    f32, bf16 = jnp.float32, jnp.bfloat16
+    parts = lax.axis_size("fsdp")
+    members = lax.axis_size("context")
+    if parts != 2:
+        grad = lax.psum_scatter(grad.astype(bf16), "fsdp", scatter_dimension=0, tiled=True)
+        return lax.psum(grad, "context")
+    core = lax.axis_index("context") % 2
+    side = lax.axis_index("fsdp")
+    model, columns = grad.shape
+    grad = grad.astype(bf16).reshape(2, 2, model // 4, columns)
+    away = lax.dynamic_slice_in_dim(grad, 1 - core, 1, 1)
+    kept = lax.dynamic_slice_in_dim(grad, core, 1, 1)
+    grad = (kept.astype(f32) + sibling(away).astype(f32)).astype(bf16)[:, 0]
+    away = lax.dynamic_slice_in_dim(grad, 1 - side, 1, 0)
+    kept = lax.dynamic_slice_in_dim(grad, side, 1, 0)
+    grad = (kept.astype(f32) + swap(away, "fsdp").astype(f32)).astype(bf16)[0]
+    groups = [list(range(c, members, 2)) for c in order]
+    grad = lax.psum(grad, "context", axis_index_groups=groups)
+    theirs = sibling(grad)
     return jnp.concatenate(
-        [
-            leading * cosine - trailing * sine_table,
-            trailing * cosine + leading * sine_table,
-            values[..., ROT:],
-        ],
-        axis=-1,
-    )
+        [jnp.where(core == 0, grad, theirs), jnp.where(core == 0, theirs, grad)], axis=0)
 
 
 def arranged_position(member, within, block_rows, members):
@@ -226,19 +274,24 @@
         start += v.size
         whole.append(jnp.moveaxis(piece, 0, -2).reshape(v.shape[:-1] + (parts * v.shape[-1],)))
     gain_a, shift_a, heads_bias, bias_o, gain_f, shift_f, up_bias, bias_d = whole
-    heads_weight = lax.all_gather(query_key_value_weight, "fsdp", axis=0, tiled=True)
-    heads_weight = heads_weight.reshape(model, 3 * width)
-    up_weight = lax.all_gather(up_projection_weight, "fsdp", axis=0, tiled=True)
-    down_weight = lax.all_gather(down_projection_weight, "fsdp", axis=1, tiled=True)
-    output_weight = lax.all_gather(attention_output_weight, "fsdp", axis=1, tiled=True)
+    heads_weight = whole_weight(query_key_value_weight.reshape(share, 3 * width), 0)
+    up_weight = whole_weight(up_projection_weight, 0)
+    output_weight = whole_weight(attention_output_weight, 1)
+    down_weight = whole_weight(down_projection_weight, 1)
 
     place = arranged_position(member, jnp.arange(rows, dtype=jnp.int32), rows, members)
     frequency = jnp.power(
         jnp.float32(rotary_base), -2.0 * jnp.arange(ROT // 2, dtype=f32) / ROT
     )
     phases = place.astype(f32)[:, None] * frequency[None, :]
-    cosine = jnp.cos(phases)[:, None, :]
-    sine = jnp.sin(phases)[:, None, :]
+    cosine, sine = jnp.cos(phases), jnp.sin(phases)
+    rest = HEAD_SIZE - ROT
+    none = jnp.zeros((rows, ROT // 2), f32)
+    blank = jnp.zeros((rows, rest), f32)
+    even = jnp.concatenate([cosine, cosine, jnp.ones((rows, rest), f32)], axis=1)
+    even = jnp.tile(even, (1, heads))[None]
+    ahead = jnp.tile(jnp.concatenate([-sine, none, blank], axis=1), (1, heads))[None]
+    behind = jnp.tile(jnp.concatenate([none, sine, blank], axis=1), (1, heads))[None]
 
     x = layer_input.astype(f32).reshape(tokens, model)
     dy_bf = cotangent.reshape(tokens, model)
@@ -250,21 +303,21 @@
     normed_f = (xhat * gain_f + shift_f).astype(bf16)
 
     projected = mm(normed_a, heads_weight, 1, 0) + heads_bias.reshape(-1)
-    projected = projected.reshape(seqs, rows, 3, width)
-    head_shape = (seqs, rows, heads, HEAD_SIZE)
-    queries = rotate(projected[:, :, 0].reshape(head_shape), cosine, sine).astype(bf16)
-    keys = rotate(projected[:, :, 1].reshape(head_shape), cosine, sine).astype(bf16)
     flat = (seqs, rows, width)
-    keys_values = jnp.stack([keys.reshape(flat), projected[:, :, 2].astype(bf16)])
+    queries, keys, values = (
+        projected[:, i * width:(i + 1) * width].reshape(flat) for i in range(3))
+    queries = rotate(queries, even, ahead, behind).astype(bf16)
+    keys = rotate(keys, even, ahead, behind).astype(bf16)
+    keys_values = jnp.stack([keys, values.astype(bf16)])
     keys_values = lax.all_gather(keys_values, "context", axis=0)
-    queries = queries.reshape(flat) * jnp.bfloat16(1.0 / math.sqrt(HEAD_SIZE))
+    queries = queries * jnp.bfloat16(1.0 / math.sqrt(HEAD_SIZE))
 
     hidden = mm(normed_f, up_weight, 1, 0) + up_bias.reshape(-1)
     gelu_output, gelu_back = jax.vjp(lambda t: jax.nn.gelu(t, approximate=False), hidden)
     activated = gelu_output.astype(bf16)
     feed_terms = mm(activated, down_weight, 1, 0)
     hidden_grad = gelu_back(mm(dy_bf, down_weight, 1, 1))[0].astype(bf16)
-    down_grad = mm(activated, dy_bf, 0, 0)
+    down_grad = mm(dy_bf, activated, 0, 0)
     up_grad = mm(normed_f, hidden_grad, 0, 0)
     up_bias_grad = jnp.sum(hidden_grad.astype(f32), axis=0)
     feed_part = mm(hidden_grad, up_weight, 1, 1)
@@ -275,76 +328,83 @@
 
     attended = attended.reshape(tokens, width)
     terms = mm(attended, output_weight, 1, 0) + feed_terms
-    branches = lax.psum(terms.astype(bf16), "tensor").astype(f32)
+    branches = sum_pair(terms.astype(bf16))
     layer_output = (x + branches + bias_o + bias_d).astype(bf16)
-    output_grad = mm(attended, dy_bf, 0, 0)
-
-    query_back = rotate(query_grad.reshape(head_shape), cosine, -sine)
-    key_back = rotate(own[0].astype(f32).reshape(head_shape), cosine, -sine)
+    output_grad = mm(dy_bf, attended, 0, 0)
+
+    query_back = rotate(query_grad, even, -ahead, -behind)
+    key_back = rotate(own[0].astype(f32), even, -ahead, -behind)
     projected_grad = jnp.concatenate(
-        [query_back.reshape(flat).astype(bf16), key_back.reshape(flat).astype(bf16), own[1]],
+        [query_back.astype(bf16), key_back.astype(bf16), own[1]],
         axis=-1,
     ).reshape(tokens, 3 * width)
     heads_grad = mm(normed_a, projected_grad, 0, 0)
     heads_bias_grad = jnp.sum(projected_grad.astype(f32), axis=0)
     heads_part = mm(projected_grad, heads_weight, 1, 1)
 
-    combined = lax.psum((heads_part * gain_a + feed_part * gain_f).astype(bf16), "tensor")
-    combined = combined.astype(f32)
+    combined = sum_pair((heads_part * gain_a + feed_part * gain_f).astype(bf16))
     input_grad = dy + scale * (
         combined
         - jnp.mean(combined, axis=-1, keepdims=True)
         - xhat * jnp.mean(combined * xhat, axis=-1, keepdims=True)
     )
 
-    def reduce_columns(grad):
-        grad = lax.psum_scatter(grad.astype(bf16), "fsdp", scatter_dimension=1, tiled=True)
-        return lax.psum(grad, "context").astype(f32)
-
-    def reduce_rows(grad):
-        grad = lax.psum_scatter(grad.astype(bf16), "fsdp", scatter_dimension=0, tiled=True)
-        return lax.psum(grad, "context").astype(f32)
-
-    up_out = reduce_rows(up_grad)
-    down_out = reduce_columns(down_grad)
-    output_out = reduce_columns(output_grad)
-    heads_out = reduce_rows(heads_grad).reshape(share, 3, width)
-
-    def by_part(v):
-        v = v.reshape(v.shape[:-1] + (parts, v.shape[-1] // parts))
-        return jnp.moveaxis(v, -2, 0).reshape(parts, -1)
-
-    shared = jnp.concatenate([by_part(v) for v in (
-        jnp.sum(heads_part * xhat, axis=0), jnp.sum(heads_part, axis=0),
-        jnp.sum(feed_part * xhat, axis=0), jnp.sum(feed_part, axis=0))], axis=1)
-    single = jnp.concatenate([by_part(v) for v in (
-        jnp.sum(dy, axis=0), heads_bias_grad.reshape(3, heads, HEAD_SIZE),
-        up_bias_grad.reshape(-1, HEAD_SIZE))], axis=1)
-    shared = lax.psum(shared, "tensor")
-    vectors = lax.psum_scatter(
-        jnp.concatenate([shared, single], axis=1), "fsdp", scatter_dimension=0, tiled=True)
-    vectors = lax.psum(vectors, "context")[0]
-    sizes = [share] * 5 + [3 * heads * HEAD_SIZE // parts, hidden_width // parts]
-    pieces = []
-    start = 0
-    for size in sizes:
-        pieces.append(vectors[start:start + size])
-        start += size
+    def as_columns(vectors):
+        flats = []
+        for v in vectors:
+            v = v.reshape(v.shape[:-1] + (parts, v.shape[-1] // parts))
+            flats.append(jnp.moveaxis(v, -2, 0).reshape(parts, -1))
+        flat_all = jnp.concatenate(flats, axis=1)
+        columns = -(-flat_all.shape[1] // share)
+        flat_all = jnp.pad(flat_all, ((0, 0), (0, columns * share - flat_all.shape[1])))
+        return jnp.moveaxis(flat_all.reshape(parts, columns, share), 1, 2).reshape(
+            model, columns)
+
+    def vectors_of(columns, sizes):
+        flat_all = columns.astype(f32).T.reshape(-1)
+        out, start = [], 0
+        for size in sizes:
+            out.append(flat_all[start:start + size])
+            start += size
+        return out
+
+    def sum_tensor(v):
+        return lax.psum(v, "tensor") if lax.axis_size("tensor") != 2 else v + swap(v, "tensor")
+
+    feed_sums = sum_tensor(jnp.stack([jnp.sum(feed_part * xhat, axis=0), jnp.sum(feed_part, axis=0)]))
+    early = as_columns([
+        feed_sums[0], feed_sums[1], jnp.sum(dy, axis=0), up_bias_grad.reshape(-1, HEAD_SIZE)])
+    early = reduce_gradient(jnp.concatenate([up_grad, down_grad, early], axis=1), (0, 1))
+    up_out = early[:, :hidden_width].astype(f32)
+    down_out = early[:, hidden_width:2 * hidden_width].astype(f32).T
+    gain_f_out, shift_f_out, bias_out, up_bias_out = vectors_of(
+        early[:, 2 * hidden_width:], [share] * 3 + [hidden_width // parts])
+
+    head_sums = sum_tensor(
+        jnp.stack([jnp.sum(heads_part * xhat, axis=0), jnp.sum(heads_part, axis=0)]))
+    late = as_columns([
+        head_sums[0], head_sums[1], heads_bias_grad.reshape(3, heads, HEAD_SIZE)])
+    late = reduce_gradient(
+        jnp.concatenate([heads_grad, output_grad, late], axis=1), (1, 0))
+    heads_out = late[:, :3 * width].astype(f32).reshape(share, 3, width)
+    output_out = late[:, 3 * width:4 * width].astype(f32).T
+    gain_a_out, shift_a_out, heads_bias_out = vectors_of(
+        late[:, 4 * width:], [share] * 2 + [3 * width // parts])
     return (
         layer_output.reshape(seqs, rows, model),
         input_grad.reshape(seqs, rows, model),
-        pieces[0],
-        pieces[1],
+        gain_a_out,
+        shift_a_out,
         heads_out,
-        pieces[5].reshape(query_key_value_bias.shape),
+        heads_bias_out.reshape(query_key_value_bias.shape),
         output_out,
-        pieces[4],
-        pieces[2],
-        pieces[3],
+        bias_out,
+        gain_f_out,
+        shift_f_out,
         up_out,
-        pieces[6].reshape(up_projection_bias.shape),
+        up_bias_out.reshape(up_projection_bias.shape),
         down_out,
-        pieces[4],
+        bias_out,
     )
 
 

time: 656 us -> 516 us (0.79)
  waiting for transfers between devices: 347 us -> 245 us
  blocking collectives: 62.6 us -> 11.9 us
  other arithmetic: 24.2 us -> 44.6 us
  starting transfers between devices: 0.7 us -> 12.6 us
  matrix products: 56.3 us -> 45 us
  local copies, waits for them, and re-layouts: 69.7 us -> 62.3 us
    ppermute x0 -> x18, waiting for transfers between devices: none -> 80.3 us  [the longest x10 75.4 us: swap(): return lax.ppermute(value, axis, [(0, 1), (1, 0)])]
    reduce_scatter x2 -> x0, waiting for transfers between devices: 64.1 us -> none  [reduce_rows(): lax.psum_scatter(grad.astype(bf16), 'fsdp', scatter_dimension=0, tiled=True)]
    unnamed x13 -> x4, waiting for transfers between devices: 40.3 us -> 0.07 us
    psum x2 -> x0, blocking collectives: 36 us -> none  [the longest x1 28 us: per_device(): vectors = lax.psum(vectors, 'context')[0]]
    reduce_scatter x1, waiting for transfers between devices: 51.3 us -> 20.7 us  [per_device(): lax.psum_scatter(kv_grad, 'context', scatter_dimension=0, tiled=True)[0]]
    psum x2, waiting for transfers between devices: 94.4 us -> 68.2 us  [reduce_gradient(): grad = lax.psum(grad, 'context', axis_index_groups=groups)]
    all_gather x3 -> x0, waiting for transfers between devices: 18 us -> none  [the longest x1 18 us: per_device(): lax.all_gather(query_key_value_weight, 'fsdp', axis=0, tiled=True)]
    reshape x11 -> x7, local copies, waits for them, and re-layouts: 17.6 us -> 4.4 us  [the longest x1 2.19 us: per_device(): heads_out = late[:, :3 * width].astype(f32).reshape(share, 3, width)]
  transfers between devices with their start and end apart: 11 -> 22, of which waited for: 9 -> 14; matrix products, arithmetic and copies ran while one was open for 16% -> 21% of each run, Pallas kernels for 11% -> 0%
where the time goes in v2:
time: 516 us; the launch traced here: 509 us
  waiting for transfers between devices  245 us (47%)
  Pallas kernels  71.1 us (14%)
  local copies, waits for them, and re-layouts  62.3 us (12%)
  matrix products  45 us (9%)
  other arithmetic  44.6 us (9%)
  between operations  16 us (3%)
  starting transfers between devices  12.6 us (2%)
  blocking collectives  11.9 us (2%)
    all_gather x1, waiting for transfers between devices, per_device(): keys_values = lax.all_gather(keys_values, 'context', axis=0)  75.9 us
    ppermute x10, waiting for transfers between devices, swap(): return lax.ppermute(value, axis, [(0, 1), (1, 0)])  75.4 us
    pallas_call x1, Pallas kernels, attention(): pl.pallas_call(lambda *refs: attention_kernel(members, half, *refs), grid...  71.1 us
    psum x2, waiting for transfers between devices, reduce_gradient(): grad = lax.psum(grad, 'context', axis_index_groups=groups)  68.2 us
    dot_general x12, matrix products, mm(): lax.dot_general(a, b, (((ca,), (cb,)), ((), ())), preferred_element_type=...  45 us
    reduce_scatter x1, waiting for transfers between devices, per_device(): lax.psum_scatter(kv_grad, 'context', scatter_dimension=0, tiled=True)[0]  20.7 us
    unnamed x148, local copies, waits for them, and re-layouts  20.5 us
    unnamed x1, blocking collectives  11.9 us
  transfers between devices with their start and end apart: 22, of which 14 were waited for; matrix products, arithmetic and copies ran while one was open for 21% of the time, Pallas kernels for 0%

profile of v2, /device:TPU:0, one launch (start us, length us, event | category | flops | bytes accessed | tf_op | source)
XLA Modules:
  0.0 508.6 jit_solution(4292435928569503122)
XLA Ops:
  7.3 2.6 copy.85
  11.2 2.9 collective-permute-start
  16.2 11.9 %all-reduce.1 = bf16[7296]{0:T(1024)(128)(2,1)S(1)} all-reduce(bf16[7296]{0:T(1024)(128)(2,1)S(1)} %dynamic-update-slice), channel_id=2, replica_groups=mesh['fsdp'=2,'context'=8,'tensor'=2] {'fsdp'}, use_global_device_ids=true, to_apply=%add.1 | all-reduce | flops 7296 | bytes 29184
  33.1 1.3 copy.92
  34.4 2.1 fusion.25
  40.5 1.8 convolution_add_fusion
  47.0 6.0 %collective-permute-done.2 = bf16[192,384]{1,0:T(8,128)(2,1)S(1)} collective-permute-done((bf16[192,384]{1,0:T(8,128)(2,1)S(1)}, bf16[192,384]{1,0:T(8,128)(2,1)S(1)}, u32[]{:S(2)}, u32[]{:S(2)}) %collective-permute-start.2) | collective-permute-done | bytes 147488 | tf_op jit(solution)/shard_map/ppermute | solution.py:173
  53.0 1.4 collective-permute-done.3
  56.3 1.5 fusion.44
  57.8 1.4 copy.95
  60.9 75.9 %all-gather.4.cloned.1.call-done = bf16[16,2,384,384]{3,2,1,0:T(8,128)(2,1)} async-done(((bf16[2,2,384,384]{3,2,1,0:T(8,128)(2,1)}), bf16[16,2,384,384]{3,2,1,0:T(8,128)(2,1)}) %all-gather.4.cloned.1.call-update) | async-done | bytes 9437200 | tf_op jit(solution)/shard_map/all_gather | solution.py:312
  136.8 71.1 %shard_map.245 = (bf16[2,384,384]{2,1,0:T(8,128)(2,1)S(1)}, f32[2,384,384]{2,1,0:T(8,128)S(1)}, bf16[8,2,2,2,192,384]{5,4,3,2,1,0:T(8,128)(2,1)}) custom-call(bf16[2,384,384]{2,1,0:T(8,128)(2,1)S(1)} %fusion.63.refs_0_, bf16[2,384,384]{2,1,0:T(8,128)(2,1)S(1)} %bitcast.182, bf16[8,2,2,2,192,384]{5,4,3,2,1,0:T(8,128)(2,1)} %bitcast.225), custom_call_target="tpu_custom_call" | custom-call | flops 12230590464 | bytes 21233664 | tf_op jit(solution)/shard_map/pallas_call | solution.py:132
  209.3 1.6 collective-permute-start.6
  212.6 13.1 %collective-permute-done.6 = bf16[768,384]{1,0:T(8,128)(2,1)} collective-permute-done((bf16[768,384]{1,0:T(8,128)(2,1)S(1)}, bf16[768,384]{1,0:T(8,128)(2,1)}, u32[]{:S(2)}, u32[]{:S(2)}) %collective-permute-start.6) | collective-permute-done | bytes 589856 | tf_op jit(solution)/shard_map/ppermute | solution.py:173
  225.6 12.0 %collective-permute-done.4 = bf16[192,1536]{1,0:T(8,128)(2,1)} collective-permute-done((bf16[192,1536]{1,0:T(8,128)(2,1)S(1)}, bf16[192,1536]{1,0:T(8,128)(2,1)}, u32[]{:S(2)}, u32[]{:S(2)}) %collective-permute-start.4) | collective-permute-done | bytes 589856 | tf_op jit(solution)/shard_map/ppermute | solution.py:173
  241.4 1.3 copy.100
  244.2 1.4 copy.99
  245.5 1.4 reshape.409
  247.0 2.4 copy.102
  249.9 2.4 copy.109
  252.3 1.5 broadcast_select_fusion.11
  253.8 1.3 broadcast_select_fusion.13
  257.7 12.8 %multiply_convert_fusion = (bf16[768,1536]{1,0:T(8,128)(2,1)}, f32[768,1536]{1,0:T(8,128)S(1)}, f32[768,1536]{1,0:T(8,128)S(1)}) fusion(f32[1536]{0:T(1024)S(1)} %copy-done.57, bf16[768,768]{1,0:T(8,128)(2,1)S(1)} %copy-done.12, bf16[384,1536]{1,0:T(8,128)(2,1)S(1)} %get-tuple-element.106, bf16[384,1536]{1,0:T(8,128)(2,1)S(1)} %get-tuple-element.105), kind=kOutput, calls=%fused_computation.13 | convolution fusion | flops 1894514688 | bytes 15341568 | tf_op jit(solution)/shard_map/dot_general | solution.py:235
  270.5 4.8 fusion.88
  276.0 1.3 copy.110
  278.1 5.4 %convolution_convert_fusion = bf16[1536,768]{0,1:T(8,128)(2,1)} fusion(bf16[768,1536]{1,0:T(8,128)(2,1)} %get-tuple-element.95, bf16[768,768]{1,0:T(8,128)(2,1)} %bitcast.192), kind=kOutput, calls=%fused_computation.28 | convolution fusion | flops 1813118976 | bytes 5898240 | tf_op jit(solution)/shard_map/dot_general | solution.py:235
  284.0 1.4 fusion.55
  285.4 20.7 %reduce-scatter.2.cloned.1.call-done = bf16[1,2,2,384,384]{4,3,2,1,0:T(8,128)(2,1)} async-done(((bf16[8,2,2,384,384]{4,3,2,1,0:T(8,128)(2,1)}), bf16[1,2,2,384,384]{4,3,2,1,0:T(8,128)(2,1)}) %reduce-scatter.2.cloned.1.call-update) | async-done | bytes 1179664 | tf_op jit(solution)/shard_map/reduce_scatter | solution.py:327
  306.1 1.4 slice_convert_fusion.1
  310.0 1.7 fusion.59
  312.4 3.8 add_convert_fusion.2
  316.2 1.5 collective-permute-start.9
  317.6 3.4 convolution_convert_fusion.1
  321.0 1.5 fusion.45
  322.5 2.1 copy.104
  324.7 1.4 fusion.79
  326.3 4.6 convolution_convert_fusion.2
  330.9 11.1 %collective-permute-done.9 = bf16[768,768]{1,0:T(8,128)(2,1)} collective-permute-done((bf16[768,768]{1,0:T(8,128)(2,1)}, bf16[768,768]{1,0:T(8,128)(2,1)}, u32[]{:S(2)}, u32[]{:S(2)}) %collective-permute-start.9) | collective-permute-done | bytes 1179680 | tf_op jit(solution)/shard_map/ppermute | solution.py:173
  342.1 3.0 fusion.37
  345.1 1.6 collective-permute-start.10
  347.3 1.5 collective-permute-done.10
  350.7 2.8 pad_maximum_fusion
  353.5 1.7 constant_dynamic-slice_fusion
  355.2 1.5 copy-done.2
  357.1 1.5 copy-done.4
  360.1 3.5 collective-permute-done.11
  363.6 2.0 add_convert_fusion.1
  365.6 1.5 collective-permute-start.12
  367.2 2.5 add_convert_fusion
  372.6 2.0 fusion.39
  374.6 1.8 add_convert_fusion.3
  377.0 5.9 %collective-permute-done.12 = bf16[1,192,1540]{2,1,0:T(8,128)(2,1)S(1)} collective-permute-done((bf16[1,192,1540]{2,1,0:T(8,128)(2,1)S(1)}, bf16[1,192,1540]{2,1,0:T(8,128)(2,1)S(1)}, u32[]{:S(2)}, u32[]{:S(2)}) %collective-permute-start.12) | collective-permute-done | bytes 591392 | tf_op jit(solution)/shard_map/ppermute | solution.py:173
  384.0 24.6 %collective-permute-done.16 = bf16[1,192,3077]{2,1,0:T(8,128)(2,1)} collective-permute-done((bf16[1,192,3077]{2,1,0:T(8,128)(2,1)}, bf16[1,192,3077]{2,1,0:T(8,128)(2,1)}, u32[]{:S(2)}, u32[]{:S(2)}) %collective-permute-start.16) | collective-permute-done | bytes 1181600 | tf_op jit(solution)/shard_map/ppermute | solution.py:173
  408.5 3.0 fusion.46
  411.6 12.3 %all-reduce.5.cloned.1.call-done = bf16[192,1540]{1,0:T(8,128)(2,1)} async-done(((bf16[192,1540]{1,0:T(8,128)(2,1)}), bf16[192,1540]{1,0:T(8,128)(2,1)}) %all-reduce.5.cloned.1.call-update) | async-done | bytes 591376 | tf_op jit(solution)/shard_map/psum | solution.py:219
  424.0 4.4 fusion.31
  428.3 55.9 %all-reduce.7.cloned.1.call-done = bf16[192,3077]{1,0:T(8,128)(2,1)} async-done(((bf16[192,3077]{1,0:T(8,128)(2,1)}), bf16[192,3077]{1,0:T(8,128)(2,1)}) %all-reduce.7.cloned.1.call-update) | async-done | bytes 1181584 | tf_op jit(solution)/shard_map/psum | solution.py:219
  484.3 1.4 broadcast_select_fusion.9
  485.7 1.3 fusion.61
  487.0 2.2 copy.107
  489.2 1.8 copy.113
  493.8 1.5 broadcast_select_fusion.1
  495.3 2.0 convert_bitcast_fusion
  499.1 1.9 copy.115
  (285 shorter events, 50.7 us)
Async XLA Ops:
  7.2 7.3 %copy-start.67 = (u32[32]{0:T(128)S(1)}, u32[32]{0:T(128)}, u32[]{:S(2)}) copy-start(u32[32]{0:T(128)} %constant.148) | copy-start | bytes 388
  7.2 7.1 %copy-start.58 = (bf16[3,6,32]{2,1,0:T(8,128)(2,1)S(1)}, bf16[3,6,32]{2,1,0:T(8,128)(2,1)}, u32[]{:S(2)}) copy-start(bf16[3,6,32]{2,1,0:T(8,128)(2,1)} %param.18) | copy-start | bytes 3460
  7.2 7.2 %copy-start.59 = (bf16[24,32]{1,0:T(8,128)(2,1)S(1)}, bf16[24,32]{1,0:T(8,128)(2,1)}, u32[]{:S(2)}) copy-start(bf16[24,32]{1,0:T(8,128)(2,1)} %param.24) | copy-start | bytes 4612
  7.2 8.5 %copy-start.61 = (bf16[384]{0:T(512)(128)(2,1)S(1)}, bf16[384]{0:T(512)(128)(2,1)}, u32[]{:S(2)}) copy-start(bf16[384]{0:T(512)(128)(2,1)} %param.15) | copy-start | bytes 2308
  7.2 8.5 %copy-start.62 = (bf16[384]{0:T(512)(128)(2,1)S(1)}, bf16[384]{0:T(512)(128)(2,1)}, u32[]{:S(2)}) copy-start(bf16[384]{0:T(512)(128)(2,1)} %param.16) | copy-start | bytes 2308
  7.2 8.5 %copy-start.63 = (bf16[384]{0:T(512)(128)(2,1)S(1)}, bf16[384]{0:T(512)(128)(2,1)}, u32[]{:S(2)}) copy-start(bf16[384]{0:T(512)(128)(2,1)} %param.20) | copy-start | bytes 2308
  7.2 8.5 %copy-start.64 = (bf16[384]{0:T(512)(128)(2,1)S(1)}, bf16[384]{0:T(512)(128)(2,1)}, u32[]{:S(2)}) copy-start(bf16[384]{0:T(512)(128)(2,1)} %param.21) | copy-start | bytes 2308
  7.3 8.5 %copy-start.65 = (bf16[384]{0:T(512)(128)(2,1)S(1)}, bf16[384]{0:T(512)(128)(2,1)}, u32[]{:S(2)}) copy-start(bf16[384]{0:T(512)(128)(2,1)} %param.22) | copy-start | bytes 2308
  7.3 8.5 %copy-start.66 = (bf16[384]{0:T(512)(128)(2,1)S(1)}, bf16[384]{0:T(512)(128)(2,1)}, u32[]{:S(2)}) copy-start(bf16[384]{0:T(512)(128)(2,1)} %param.26) | copy-start | bytes 2308
  7.3 21.6 %copy-start = (bf16[2,384,768]{2,1,0:T(8,128)(2,1)S(1)}, bf16[2,384,768]{2,1,0:T(8,128)(2,1)}, u32[]{:S(2)}) copy-start(bf16[2,384,768]{2,1,0:T(8,128)(2,1)} %param.14) | copy-start | bytes 3538948
  7.3 129.5 %all-gather.4.cloned.1.call-start = ((), (), s32[]{:S(2)}) async-start(), calls=%async_computation.4 | async-start | bytes 10616832 | tf_op jit(solution)/shard_map/all_gather | solution.py:312
  11.2 19.6 %collective-permute-start = (bf16[192,1152]{1,0:T(8,128)(2,1)}, bf16[192,1152]{1,0:T(8,128)(2,1)}, u32[]{:S(2)}, u32[]{:S(2)}) collective-permute-start(bf16[192,1152]{1,0:T(8,128)(2,1)} %copy.86), channel_id=1, source_target_pairs={{0,16},{16,0},{1,17},{17,1},{2,18},{18,2},{3,19},{19,3},{4,20},{20... | collective-permute-start | bytes 1327112 | tf_op jit(solution)/shard_map/ppermute | solution.py:173
  30.3 4.1 copy-start.49
  30.8 5.7 %copy-start.51 = (f32[768]{0:T(1024)}, f32[768]{0:T(1024)S(1)}, u32[]{:S(2)}) copy-start(f32[768]{0:T(1024)S(1)} %reshape.407) | copy-start | bytes 9220
  30.8 6.9 %collective-permute-start.1 = (bf16[192,1152]{1,0:T(8,128)(2,1)}, bf16[192,1152]{1,0:T(8,128)(2,1)}, u32[]{:S(2)}, u32[]{:S(2)}) collective-permute-start(bf16[192,1152]{1,0:T(8,128)(2,1)} %collective-permute-done), channel_id=1, source_target_pairs={{0,2},{2,0},{4,6},{6,4},{8,10},{10,8},{12,14},{14,12},{1,3},{3,1},... | collective-permute-start | bytes 1327112 | tf_op jit(solution)/shard_map/ppermute | solution.py:178
  44.3 12.0 %copy-start.8 = (bf16[2,384,768]{2,1,0:T(8,128)(2,1)S(1)}, bf16[2,384,768]{2,1,0:T(8,128)(2,1)}, u32[]{:S(2)}) copy-start(bf16[2,384,768]{2,1,0:T(8,128)(2,1)} %param.27) | copy-start | bytes 3538948
  45.5 260.6 %reduce-scatter.2.cloned.1.call-start = ((), (), s32[]{:S(2)}) async-start(), calls=%async_computation.1 | async-start | bytes 10616832 | tf_op jit(solution)/shard_map/reduce_scatter | solution.py:327
  46.6 6.3 %collective-permute-start.2 = (bf16[192,384]{1,0:T(8,128)(2,1)S(1)}, bf16[192,384]{1,0:T(8,128)(2,1)S(1)}, u32[]{:S(2)}, u32[]{:S(2)}) collective-permute-start(bf16[192,384]{1,0:T(8,128)(2,1)S(1)} %constant_dynamic-slice_fusion.4), channel_id=1, source_target_pairs={{0,16},{16,0},{1,17},{17,1},{2,18},{18,2},{3,19},{19,3},{4,20},{20... | collective-permute-start | bytes 442376 | tf_op jit(solution)/shard_map/ppermute | solution.py:173
  53.0 1.4 collective-permute-start.3
  208.0 31.3 %copy-start.9 = (bf16[2,384,768]{2,1,0:T(8,128)(2,1)S(1)}, bf16[2,384,768]{2,1,0:T(8,128)(2,1)}, u32[]{:S(2)}) copy-start(bf16[2,384,768]{2,1,0:T(8,128)(2,1)} %param.27) | copy-start | bytes 3538948
  208.0 215.9 %all-reduce.5.cloned.1.call-start = ((), (), s32[]{:S(2)}) async-start(), calls=%async_computation.2 | async-start | bytes 1277952 | tf_op jit(solution)/shard_map/psum | solution.py:219
  208.1 29.5 %copy-start.47 = (f32[384,64]{0,1:T(8,128)S(1)}, f32[384,64]{0,1:T(8,128)}, u32[]{:S(2)}) copy-start(f32[384,64]{0,1:T(8,128)} %copy-done.46) | copy-start | bytes 294916
  208.1 30.4 %copy-start.45 = (f32[384,64]{0,1:T(8,128)S(1)}, f32[384,64]{0,1:T(8,128)}, u32[]{:S(2)}) copy-start(f32[384,64]{0,1:T(8,128)} %copy-done.44) | copy-start | bytes 294916
  209.3 16.3 %collective-permute-start.6 = (bf16[768,384]{1,0:T(8,128)(2,1)S(1)}, bf16[768,384]{1,0:T(8,128)(2,1)}, u32[]{:S(2)}, u32[]{:S(2)}) collective-permute-start(bf16[768,384]{1,0:T(8,128)(2,1)S(1)} %constant_dynamic-slice_fusion.2), channel_id=1, source_target_pairs={{0,16},{16,0},{1,17},{17,1},{2,18},{18,2},{3,19},{19,3},{4,20},{20... | collective-permute-start | bytes 1769480 | tf_op jit(solution)/shard_map/ppermute | solution.py:173
  212.0 25.6 %collective-permute-start.4 = (bf16[192,1536]{1,0:T(8,128)(2,1)S(1)}, bf16[192,1536]{1,0:T(8,128)(2,1)}, u32[]{:S(2)}, u32[]{:S(2)}) collective-permute-start(bf16[192,1536]{1,0:T(8,128)(2,1)S(1)} %constant_dynamic-slice_fusion.3), channel_id=1, source_target_pairs={{0,16},{16,0},{1,17},{17,1},{2,18},{18,2},{3,19},{19,3},{4,20},{20... | collective-permute-start | bytes 1769480 | tf_op jit(solution)/shard_map/ppermute | solution.py:173
  225.6 26.7 %collective-permute-start.7 = (bf16[768,384]{1,0:T(8,128)(2,1)}, bf16[768,384]{1,0:T(8,128)(2,1)}, u32[]{:S(2)}, u32[]{:S(2)}) collective-permute-start(bf16[768,384]{1,0:T(8,128)(2,1)} %collective-permute-done.6), channel_id=1, source_target_pairs={{0,2},{2,0},{4,6},{6,4},{8,10},{10,8},{12,14},{14,12},{1,3},{3,1},... | collective-permute-start | bytes 1769480 | tf_op jit(solution)/shard_map/ppermute | solution.py:178
  237.6 16.2 %collective-permute-start.5 = (bf16[192,1536]{1,0:T(8,128)(2,1)}, bf16[192,1536]{1,0:T(8,128)(2,1)}, u32[]{:S(2)}, u32[]{:S(2)}) collective-permute-start(bf16[192,1536]{1,0:T(8,128)(2,1)} %collective-permute-done.4), channel_id=1, source_target_pairs={{0,2},{2,0},{4,6},{6,4},{8,10},{10,8},{12,14},{14,12},{1,3},{3,1},... | collective-permute-start | bytes 1769480 | tf_op jit(solution)/shard_map/ppermute | solution.py:178
  244.2 5.2 %copy-start.55 = (bf16[768]{0:T(1024)(128)(2,1)S(1)}, bf16[768]{0:T(1024)(128)(2,1)}, u32[]{:S(2)}) copy-start(bf16[768]{0:T(1024)(128)(2,1)} %reduce.4) | copy-start | bytes 4612
  256.9 13.5 %copy-start.27 = (bf16[1536,384]{1,0:T(8,128)(2,1)}, bf16[1536,384]{1,0:T(8,128)(2,1)S(1)}, u32[]{:S(2)}) copy-start(bf16[1536,384]{1,0:T(8,128)(2,1)S(1)} %get-tuple-element.103) | copy-start | bytes 3538948
  256.9 13.5 %copy-start.29 = (bf16[1536,384]{1,0:T(8,128)(2,1)}, bf16[1536,384]{1,0:T(8,128)(2,1)S(1)}, u32[]{:S(2)}) copy-start(bf16[1536,384]{1,0:T(8,128)(2,1)S(1)} %get-tuple-element.104) | copy-start | bytes 3538948
  257.7 12.8 %copy-start.10 = (bf16[2,384,768]{2,1,0:T(8,128)(2,1)S(1)}, bf16[2,384,768]{2,1,0:T(8,128)(2,1)}, u32[]{:S(2)}) copy-start(bf16[2,384,768]{2,1,0:T(8,128)(2,1)} %param.27) | copy-start | bytes 3538948
  308.7 3.0 copy-start.18
  311.7 4.5 copy-start.22
  312.4 5.3 %copy-start.39 = (bf16[768,768]{1,0:T(8,128)(2,1)S(1)}, bf16[768,768]{1,0:T(8,128)(2,1)}, u32[]{:S(2)}) copy-start(bf16[768,768]{1,0:T(8,128)(2,1)} %copy.109) | copy-start | bytes 3538948
  316.2 25.9 %collective-permute-start.9 = (bf16[768,768]{1,0:T(8,128)(2,1)}, bf16[768,768]{1,0:T(8,128)(2,1)}, u32[]{:S(2)}, u32[]{:S(2)}) collective-permute-start(bf16[768,768]{1,0:T(8,128)(2,1)} %get-tuple-element.156), channel_id=1, source_target_pairs={{0,1},{1,0},{2,3},{3,2},{4,5},{5,4},{6,7},{7,6},{8,9},{9,8},{10,11... | collective-permute-start | bytes 3538952 | tf_op jit(solution)/shard_map/ppermute | solution.py:173
  317.6 3.4 copy-start.11
  321.0 3.6 copy-start.19
  321.0 5.2 %copy-start.17 = (bf16[2,384,384]{2,1,0:T(8,128)(2,1)S(1)}, bf16[2,384,384]{2,1,0:T(8,128)(2,1)}, u32[]{:S(2)}) copy-start(bf16[2,384,384]{2,1,0:T(8,128)(2,1)} %fusion.55) | copy-start | bytes 1769476
  326.2 15.8 %copy-start.1 = (bf16[2,384,768]{2,1,0:T(8,128)(2,1)S(1)}, bf16[2,384,768]{2,1,0:T(8,128)(2,1)}, u32[]{:S(2)}) copy-start(bf16[2,384,768]{2,1,0:T(8,128)(2,1)} %param.14) | copy-start | bytes 3538948
  326.2 15.8 %copy-start.23 = (f32[768,768]{1,0:T(8,128)S(1)}, f32[768,768]{1,0:T(8,128)}, u32[]{:S(2)}) copy-start(f32[768,768]{1,0:T(8,128)} %copy-done.22) | copy-start | bytes 7077892
  326.3 15.8 %copy-start.24 = (f32[768,768]{1,0:T(8,128)S(1)}, f32[768,768]{1,0:T(8,128)}, u32[]{:S(2)}) copy-start(f32[768,768]{1,0:T(8,128)} %get-tuple-element.157) | copy-start | bytes 7077892
  342.0 8.4 %copy-start.60 = (bf16[2,384]{1,0:T(2,128)(2,1)S(1)}, bf16[2,384]{1,0:T(2,128)(2,1)}, u32[]{:S(2)}) copy-start(bf16[2,384]{1,0:T(2,128)(2,1)} %reshape.400) | copy-start | bytes 4612
  345.1 3.7 collective-permute-start.10
  346.7 3.7 collective-permute-start.14
  353.5 3.2 copy-start.2
  353.5 3.2 copy-start.20
  353.5 3.3 copy-start.25
  356.7 10.4 %collective-permute-start.15 = (bf16[2,1,192,3077]{3,2,1,0:T(8,128)(2,1)}, bf16[2,1,192,3077]{3,2,1,0:T(8,128)(2,1)}, u32[]{:S(2)}, u32[]{:S(2)}) collective-permute-start(bf16[2,1,192,3077]{3,2,1,0:T(8,128)(2,1)} %constant_dynamic-slice_fusion), channel_id=1, source_target_pairs={{0,2},{2,0},{4,6},{6,4},{8,10},{10,8},{12,14},{14,12},{1,3},{3,1},... | collective-permute-start | bytes 7089416 | tf_op jit(solution)/shard_map/ppermute | solution.py:178
  359.7 3.9 collective-permute-start.11
  360.1 7.1 %copy-start.3 = (bf16[2,2,192,3077]{3,2,1,0:T(8,128)(2,1)S(1)}, bf16[2,2,192,3077]{3,2,1,0:T(8,128)(2,1)}, u32[]{:S(2)}) copy-start(bf16[2,2,192,3077]{3,2,1,0:T(8,128)(2,1)} %copy-done.2) | copy-start | bytes 14178820
  365.6 17.3 %collective-permute-start.12 = (bf16[1,192,1540]{2,1,0:T(8,128)(2,1)S(1)}, bf16[1,192,1540]{2,1,0:T(8,128)(2,1)S(1)}, u32[]{:S(2)}, u32[]{:S(2)}) collective-permute-start(bf16[1,192,1540]{2,1,0:T(8,128)(2,1)S(1)} %dynamic-slice_bitcast_fusion.1), channel_id=1, source_target_pairs={{0,16},{16,0},{1,17},{17,1},{2,18},{18,2},{3,19},{19,3},{4,20},{20... | collective-permute-start | bytes 1774088 | tf_op jit(solution)/shard_map/ppermute | solution.py:173
  367.2 4.2 copy-start.69
  369.6 5.0 copy-start.5
  369.7 2.9 copy-start.30
  370.8 3.8 copy-start.36
  370.8 3.8 copy-start.38
  370.8 37.7 %collective-permute-start.16 = (bf16[1,192,3077]{2,1,0:T(8,128)(2,1)}, bf16[1,192,3077]{2,1,0:T(8,128)(2,1)}, u32[]{:S(2)}, u32[]{:S(2)}) collective-permute-start(bf16[1,192,3077]{2,1,0:T(8,128)(2,1)} %dynamic-slice_bitcast_fusion), channel_id=1, source_target_pairs={{0,16},{16,0},{1,17},{17,1},{2,18},{18,2},{3,19},{19,3},{4,20},{20... | collective-permute-start | bytes 3544712 | tf_op jit(solution)/shard_map/ppermute | solution.py:173
  376.4 47.5 %collective-permute-start.8 = (bf16[768,768]{1,0:T(8,128)(2,1)}, bf16[768,768]{1,0:T(8,128)(2,1)}, u32[]{:S(2)}, u32[]{:S(2)}) collective-permute-start(bf16[768,768]{1,0:T(8,128)(2,1)} %add_convert_fusion.3), channel_id=1, source_target_pairs={{0,1},{1,0},{2,3},{3,2},{4,5},{5,4},{6,7},{7,6},{8,9},{9,8},{10,11... | collective-permute-start | bytes 3538952 | tf_op jit(solution)/shard_map/ppermute | solution.py:173
  383.9 27.7 %copy-start.54 = (f32[2,384]{1,0:T(2,128)S(1)}, f32[2,384]{1,0:T(2,128)}, u32[]{:S(2)}) copy-start(f32[2,384]{1,0:T(2,128)} %get-tuple-element.145) | copy-start | bytes 9220
  383.9 27.7 %copy-start.53 = (f32[2,384]{1,0:T(2,128)S(1)}, f32[2,384]{1,0:T(2,128)}, u32[]{:S(2)}) copy-start(f32[2,384]{1,0:T(2,128)} %get-tuple-element.144) | copy-start | bytes 9220
  383.9 100.3 %all-reduce.7.cloned.1.call-start = ((), (), s32[]{:S(2)}) async-start(), calls=%async_computation.3 | async-start | bytes 2457600 | tf_op jit(solution)/shard_map/psum | solution.py:219
  423.9 60.3 %collective-permute-start.13 = (bf16[192,1540]{1,0:T(8,128)(2,1)}, bf16[192,1540]{1,0:T(8,128)(2,1)}, u32[]{:S(2)}, u32[]{:S(2)}) collective-permute-start(bf16[192,1540]{1,0:T(8,128)(2,1)} %all-reduce.5.cloned.1.call-done), channel_id=1, source_target_pairs={{0,2},{2,0},{4,6},{6,4},{8,10},{10,8},{12,14},{14,12},{1,3},{3,1},... | collective-permute-start | bytes 1774088 | tf_op jit(solution)/shard_map/ppermute | solution.py:178
  484.2 9.5 %collective-permute-start.17 = (bf16[192,3077]{1,0:T(8,128)(2,1)}, bf16[192,3077]{1,0:T(8,128)(2,1)}, u32[]{:S(2)}, u32[]{:S(2)}) collective-permute-start(bf16[192,3077]{1,0:T(8,128)(2,1)} %all-reduce.7.cloned.1.call-done), channel_id=1, source_target_pairs={{0,2},{2,0},{4,6},{6,4},{8,10},{10,8},{12,14},{14,12},{1,3},{3,1},... | collective-permute-start | bytes 3544712 | tf_op jit(solution)/shard_map/ppermute | solution.py:178
  498.2 2.9 copy-start.56
  (28 other events, 45.5 us)
Sparse Core Ops, SparseCore 0:
  45.6 91.1 all-gather.3
  208.1 97.9 reduce-scatter.1
  384.0 39.8 all-reduce.4
  426.8 57.3 all-reduce.6
